TPU v7x, 512 devices: a whole 4x8x8 slice. The times are simulated.
512 devices in a mesh: node: 32 (over z, x), dev: 16 (over y, core).
Axes of the slice: x: 4, y: 8, z: 8, core: 2. Of those that a mesh axis runs over, the one named last changes fastest.
Arguments:
- tokens: bfloat16 [65536, 8192], P(('node', 'dev')), may hold values from -24 to 24
- queries: bfloat16 [65536, 1024], P(('node', 'dev')), may hold values from -20 to 20
- grad_out: bfloat16 [65536, 1024], P(('node', 'dev')), may hold values from -6 to 6
- seg_ids: int32 [512, 128], P(('node', 'dev')), may hold values from 0 to 3, never falling along the last dimension, each value on 1 to 64 neighbouring positions
- w_values: bfloat16 [8192, 256], P(('node', 'dev')), may hold values from -0.0625 to 0.0625
- w_scales: bfloat16 [4], replicated, may hold values from 0.5 to 2
Outputs:
- attn_out: bfloat16 [65536, 1024], P(('node', 'dev'))
- grad_tokens: bfloat16 [65536, 8192], P(('node', 'dev'))
- grad_weight: float32 [8192, 256], P(('node', 'dev'))
Inputs may be any that keep to these rules, and one draw needn't show every extreme that they name: `seg_ids`: each device's document numbers never fall along its tokens, each document holds 1 to 64 tokens and one holds exactly that many.
All inputs are finite; a program needn't handle non-finite values.
Results may differ from a plain program's by a relative error of at most 0.024.
Values may be sent and summed in bfloat16 or wider, within the bound.
A program may use at most 64 MiB of HBM per device.

v0:
```python
import jax
import jax.numpy as jnp
from jax import lax
from jax.sharding import PartitionSpec as P

HD = 128
GH = 8
GROUPS = 1
RB = 2048


def dequantize(stored, scales):
    rows_all, cols_all = stored.shape
    grouped = stored.reshape(rows_all // RB, RB, cols_all).astype(jnp.float32)
    scaled = grouped * scales.astype(jnp.float32)[:, None, None]
    return scaled.reshape(rows_all, cols_all).astype(jnp.bfloat16)


def attend(queries, keys, values, segments, cotangent):
    count = queries.shape[0]
    query_heads = queries.reshape(count, GROUPS, GH, HD)
    key_heads = keys.reshape(count, GROUPS, HD)
    value_heads = values.reshape(count, GROUPS, HD)
    score_scale = HD ** (-0.5)
    scores = (
        jnp.einsum("tgha,sga->ghts", query_heads, key_heads, preferred_element_type=jnp.float32)
        * score_scale
    )
    positions = jnp.arange(count)
    allowed = (positions[None, :] <= positions[:, None]) & (segments[:, None] == segments[None, :])
    scores = jnp.where(allowed, scores, -1e30)
    row_top = jnp.max(scores, axis=-1, keepdims=True)
    expanded = jnp.where(allowed, jnp.exp(scores - row_top), 0.0)
    probability = expanded / jnp.sum(expanded, axis=-1, keepdims=True)
    probs_low = probability.astype(jnp.bfloat16)
    attended = jnp.einsum(
        "ghts,sga->tgha", probs_low, value_heads, preferred_element_type=jnp.float32
    )
    attended = attended.reshape(count, -1).astype(jnp.bfloat16)
    cot_heads = cotangent.reshape(count, GROUPS, GH, HD)
    grad_values = jnp.einsum(
        "ghts,tgha->sga", probs_low, cot_heads, preferred_element_type=jnp.float32
    )
    grad_probs = jnp.einsum(
        "tgha,sga->ghts", cot_heads, value_heads, preferred_element_type=jnp.float32
    )
    inner = jnp.sum(probability * grad_probs, axis=-1, keepdims=True)
    grad_scores = (probability * (grad_probs - inner) * score_scale).astype(jnp.bfloat16)
    grad_keys = jnp.einsum(
        "ghts,tgha->sga", grad_scores, query_heads, preferred_element_type=jnp.float32
    )
    grad_kv = jnp.concatenate(
        [grad_keys.reshape(count, -1), grad_values.reshape(count, -1)], axis=1
    )
    return (attended, grad_kv.astype(jnp.bfloat16))


def shards(tokens, queries, grad_out, seg_ids, w_values, w_scales):
    full_values = lax.all_gather(w_values, ("node", "dev"), axis=0, tiled=True)
    weight = dequantize(full_values, w_scales)
    key_width = GROUPS * HD
    keys_values = jnp.dot(tokens, weight, preferred_element_type=jnp.float32).astype(jnp.bfloat16)
    attn_out, grad_kv = attend(
        queries, keys_values[:, :key_width], keys_values[:, key_width:], seg_ids[0], grad_out
    )
    grad_tokens = lax.dot_general(
        grad_kv, weight, (((1,), (1,)), ((), ())), preferred_element_type=jnp.float32
    ).astype(jnp.bfloat16)
    node_count = lax.axis_size("node")
    dev_count = lax.axis_size("dev")
    columns = grad_kv.shape[1]
    width = tokens.shape[1]
    slice_rows = width // (node_count * dev_count)
    partial_value = lax.dot_general(
        tokens, grad_kv, (((0,), (0,)), ((), ())), preferred_element_type=jnp.float32
    ).astype(jnp.bfloat16)
    blocks = partial_value.reshape(node_count, dev_count, slice_rows, columns)
    received = lax.all_to_all(blocks, "dev", split_axis=1, concat_axis=1, tiled=True)
    node_group = jnp.sum(received.astype(jnp.float32), axis=1).astype(jnp.bfloat16)
    owned_rows = lax.psum_scatter(
        node_group.astype(jnp.float32).astype(jnp.bfloat16), "node", scatter_dimension=0, tiled=True
    ).astype(jnp.float32)
    grad_weight = owned_rows.reshape(-1, columns)
    return (attn_out, grad_tokens, grad_weight)


def solution(mesh):
    return jax.shard_map(
        shards,
        mesh=mesh,
        in_specs=(
            P(("node", "dev"), None),
            P(("node", "dev"), None),
            P(("node", "dev"), None),
            P(("node", "dev"), None),
            P(("node", "dev"), None),
            P(),
        ),
        out_specs=(P(("node", "dev"), None), P(("node", "dev"), None), P(("node", "dev"), None)),
        check_vma=False,
    )
```

profile of v0, /device:TPU:1, one launch (start us, length us, event | category | flops | bytes accessed | tf_op | source)
XLA Modules:
  0.0 475.0 jit_solution(16199251408865016666)
XLA Ops:
  7.2 0.7 all-gather.2.cloned.1.call-update
  7.9 0.0 reduce-scatter.2.cloned.1.call-start
  8.0 0.7 convert_element_type.50
  8.6 0.1 broadcast_bitcast_fusion
  8.7 1.1 copy.49
  9.8 1.1 copy.50
  11.0 0.8 fusion.18
  11.8 125.0 %all-gather.2.cloned.1.call-done = bf16[8192,256]{1,0:T(8,128)(2,1)} async-done(((bf16[16,256]{1,0:T(8,128)(2,1)}), bf16[8192,256]{1,0:T(8,128)(2,1)}) %all-gather.2.cloned.1.call-update) | async-done | bytes 4194320 | tf_op jit(solution)/shard_map/all_gather | solution.py:59
  136.8 4.6 fusion.5
  141.4 0.3 fusion.25
  141.7 0.1 fusion.9
  141.8 0.3 fusion.7
  142.1 0.3 multiply_reduce_fusion
  142.3 0.3 fusion.6
  142.7 3.2 fusion
  145.9 6.4 %copy.39 = bf16[8192,256]{1,0:T(8,128)(2,1)} copy(bf16[8192,256]{0,1:T(8,128)(2,1)} %fusion) | data formatting | bytes 8388608 | tf_op jit(solution)/shard_map/convert_element_type | solution.py:76
  152.3 2.6 copy.40
  154.9 100.2 %all_to_all.5 = bf16[32,16,16,256]{3,2,0,1:T(8,128)(2,1)} all-to-all(bf16[32,16,16,256]{3,2,0,1:T(8,128)(2,1)S(1)} %copy.40), channel_id=1, replica_groups=mesh['node'=32,'dev'=16] {'dev'}, dimensions={1} | all-to-all | bytes 8388608 | tf_op jit(solution)/shard_map/all_to_all | solution.py:78
  255.1 3.6 reduce_sum.32
  258.7 0.3 convolution_convert_fusion.2
  259.0 0.9 copy.41
  259.8 4.7 convolution_convert_fusion.1
  264.5 202.4 %reduce-scatter.2.cloned.1.call-done = bf16[1,16,256]{2,1,0:T(8,128)(2,1)} async-done(((bf16[32,16,256]{2,1,0:T(8,128)(2,1)}), bf16[1,16,256]{2,1,0:T(8,128)(2,1)}) %reduce-scatter.2.cloned.1.call-update) | async-done | bytes 8208 | tf_op jit(solution)/shard_map/reduce_scatter | solution.py:80
  466.9 1.3 bitcast_convert_fusion
  (5 shorter events, 0.1 us)
Async XLA Ops:
  7.2 129.6 %copy-start = (bf16[128,8192]{1,0:T(8,128)(2,1)S(1)}, bf16[128,8192]{1,0:T(8,128)(2,1)}, u32[]{:S(2)}) copy-start(bf16[128,8192]{1,0:T(8,128)(2,1)} %param.6) | copy-start | bytes 6291460
  7.2 129.6 %all-gather.2.cloned.1.call-start = ((), (), s32[]{:S(2)}) async-start(), calls=%async_computation.2 | async-start | bytes 4202496 | tf_op jit(solution)/shard_map/all_gather | solution.py:59
  7.9 459.0 %reduce-scatter.2.cloned.1.call-start = ((), (), s32[]{:S(2)}) async-start(), calls=%async_computation.3 | async-start | bytes 270336 | tf_op jit(solution)/shard_map/reduce_scatter | solution.py:80
Sparse Core Ops, SparseCore 0:
  12.2 124.5 all-gather.1
  258.8 208.0 reduce-scatter.1
where the time goes:
time: 480 us; the launch traced here: 475 us
  waiting for transfers between devices  328 us (68%)
  blocking collectives  100 us (21%)
  between operations  14.1 us (3%)
  matrix products  14 us (3%)
  local copies, waits for them, and re-layouts  12.2 us (3%)
  other arithmetic  6.44 us (1%)
    reduce_scatter x1, waiting for transfers between devices, shards(): lax.psum_scatter(node_group.astype(jnp.float32).astype(jnp.bfloat16), 'no...  202 us
    all_gather x1, waiting for transfers between devices, shards(): full_values = lax.all_gather(w_values, ('node', 'dev'), axis=0, tiled=True)  125 us
    all_to_all x1, blocking collectives, shards(): lax.all_to_all(blocks, 'dev', split_axis=1, concat_axis=1, tiled=True)  100 us
  transfers between devices with their start and end apart: 2, of which 2 were waited for; matrix products, arithmetic and copies ran while one was open for 2% of the time, Pallas kernels for 0%

commit v1 on v0

v1 whole, which is shorter than its diff:
```python
import functools
import jax
import jax.numpy as jnp
from jax import lax
from jax.experimental import pallas as pl
from jax.experimental.pallas import tpu as pltpu
from jax.sharding import PartitionSpec as P

HD = 128
GH = 8
NX, NY, NZ = 4, 8, 8
TOK = 128
D = 8192
HALF = D // 2
BLK = HALF // NZ
SCALE = HD ** (-0.5)
MESH = pl.DeviceIdType.MESH
F32, BF16 = jnp.float32, jnp.bfloat16
NT = (((1,), (1,)), ((), ()))
TN = (((0,), (0,)), ((), ()))
NN = (((1,), (0,)), ((), ()))


def dot(a, b, dims=NN):
    return lax.dot_general(a, b, dims, preferred_element_type=F32)


def wait_bytes(ref, sem):
    pltpu.make_async_copy(ref, ref, sem).wait()


def kernel(
    tok, q_hbm, go_hbm, seg, w, scales,
    attn, gtok, gw,
    X, XT, W, GT, qv, gov, plow_s, sh, kvs, kvr, G, SB, RB, YS, YR, XS, XR,
    l_sem, tok_sem, ag_x_send, ag_x_recv, ag_d_send, ag_d_recv, ag_send, ag_recv,
    kv_sem, g_sem, gt_sem, rs_send, rs_recv, rs_d_send, rs_d_recv, rs_x_send, rs_x_recv,
):
    node, dev = lax.axis_index("node"), lax.axis_index("dev")
    z, x = node // NX, node % NX
    y, c = dev // 2, dev % 2
    other = 1 - c

    def at(x, y, z, c):
        return {"node": z * NX + x, "dev": y * 2 + c}

    def remote(src, dst, ss, rs, target):
        return pltpu.make_async_remote_copy(
            src_ref=src, dst_ref=dst, send_sem=ss, recv_sem=rs, device_id=target, device_id_type=MESH
        )

    def cols(zz, core):
        return pl.ds(pl.multiple_of(zz * 2 * BLK + core * BLK, BLK), BLK)

    mine = pl.ds(pl.multiple_of(c * TOK, TOK), TOK)
    theirs = pl.ds(pl.multiple_of(other * TOK, TOK), TOK)

    bar = pltpu.get_barrier_semaphore()
    for k in range(1, 2 * NX):
        xx = (x + k // 2) % NX
        cc = (c + k % 2) % 2
        pl.semaphore_signal(bar, inc=1, device_id=at(xx, y, z, cc), device_id_type=MESH)
    for k in range(1, NY):
        pl.semaphore_signal(bar, inc=1, device_id=at(x, (y + k) % NY, z, c), device_id_type=MESH)
    for k in range(1, NZ):
        pl.semaphore_signal(bar, inc=1, device_id=at(x, y, (z + k) % NZ, c), device_id_type=MESH)

    for zz in range(NZ):
        pltpu.make_async_copy(tok.at[:, cols(zz, c)], X.at[zz, mine], l_sem.at[0]).start()
    q_copy = pltpu.make_async_copy(q_hbm, qv, l_sem.at[1])
    go_copy = pltpu.make_async_copy(go_hbm, gov, l_sem.at[2])
    q_copy.start()
    go_copy.start()

    pick = lax.broadcasted_iota(jnp.int32, (1, 4), 1) == z // 2
    scale = jnp.sum(jnp.where(pick, scales[...].astype(F32), 0.0), axis=1, keepdims=True)
    scaled = (w[...].astype(F32) * scale).astype(BF16)
    sh[0] = scaled[:, :HD]
    sh[1] = scaled[:, HD:]

    pl.semaphore_wait(bar, 2 * NX - 1 + NY - 1 + NZ - 1)

    def x_targets():
        for k in range(NX):
            yield k, (x + k) % NX

    home = x // 2
    for p in range(2):
        def own_place(p=p):
            return W.at[p, z, x % 2, y, pl.ds(pl.multiple_of(c * 16, 16), 16)]

        for k, xx in x_targets():
            cp = remote(sh.at[p], own_place(), ag_x_send.at[p, k], ag_x_recv.at[p], at(xx, y, z, home))
            if k == 0:
                @pl.when(home != c)
                def _():
                    cp.start()

                @pl.when(home == c)
                def _():
                    pltpu.make_async_copy(sh.at[p], own_place(), ag_x_recv.at[p]).start()
            else:
                cp.start()

    for zz in range(NZ):
        remote(tok.at[:, cols(zz, other)], X.at[zz, mine], tok_sem.at[0], tok_sem.at[1], at(x, y, z, other)).start()

    wait_bytes(W.at[0, z, :, y], ag_x_recv.at[0])
    for k in range(1, NY):
        remote(W.at[0, z, :, y], W.at[0, z, :, y], ag_d_send.at[0], ag_d_recv.at[0], at(x, (y + k) % NY, z, c)).start()
    wait_bytes(W.at[1, z, :, y], ag_x_recv.at[1])
    for k in range(1, NZ):
        remote(W.at[1, z, :, y], W.at[1, z, :, y], ag_d_send.at[1], ag_d_recv.at[1], at(x, y, (z + k) % NZ, c)).start()

    wait_bytes(X.at[:, mine], l_sem.at[0])
    wait_bytes(X.at[:, theirs], tok_sem.at[1])

    def turn(zz):
        XT[zz] = X[zz].T

    def piece(p, i, sub):
        if p == 0:
            return W.at[0, i, sub]
        return W.at[1, pl.ds(sub * (NZ // 2), NZ // 2), :, i]

    def ring(p):
        return (z, NZ) if p == 0 else (y, NY)

    def neighbour(p, step):
        if p == 0:
            return at(x, y, (z + step + NZ) % NZ, c)
        return at(x, (y + step + NY) % NY, z, c)

    def ag_copy(p, d, s, sub):
        pos, n = ring(p)
        step = 1 - 2 * d
        i = (pos - step * (s - 1) + n) % n
        return remote(piece(p, i, sub), piece(p, i, sub), ag_send.at[p, d, s - 1, sub], ag_recv.at[p, d, s - 1, sub], neighbour(p, step))

    def ag_arrival(p, d, s, sub):
        pos, n = ring(p)
        step = 1 - 2 * d
        i = (pos - step * s + n) % n
        wait_bytes(piece(p, i, sub), ag_recv.at[p, d, s - 1, sub])

    wait_bytes(W.at[0, pl.ds(0, NY - 1), :, 0], ag_d_recv.at[0])
    for sub in range(2):
        for d in range(2):
            ag_copy(0, d, 1, sub).start()
    wait_bytes(W.at[1, pl.ds(0, NZ - 1), :, 0], ag_d_recv.at[1])
    for sub in range(2):
        for d in range(2):
            ag_copy(1, d, 1, sub).start()
    for s in range(2, 5):
        for zz in range((s - 2) * 3, min((s - 1) * 3, NZ)):
            turn(zz)
        for sub in range(2):
            for p in range(2):
                for d in range(2):
                    ag_arrival(p, d, s - 1, sub)
                    if s < 4 or sub == d:
                        ag_copy(p, d, s, sub).start()
    for p in range(2):
        for d in range(2):
            ag_arrival(p, d, 4, d)

    acc = jnp.zeros((2 * TOK, 2 * HD), F32)
    for zz in range(NZ):
        wz = jnp.concatenate([W[0, zz].reshape(BLK, HD), W[1, zz].reshape(BLK, HD)], axis=1)
        acc += dot(X[zz], wz)
    kvs[...] = acc
    kv_copy = remote(kvs.at[theirs], kvr, kv_sem.at[0], kv_sem.at[1], at(x, y, z, other))
    kv_copy.start()

    seg_t = jnp.broadcast_to(seg[...].astype(F32), (TOK, TOK))
    seg_s = seg_t.T
    s_at = lax.broadcasted_iota(jnp.int32, (TOK, TOK), 0)
    t_at = lax.broadcasted_iota(jnp.int32, (TOK, TOK), 1)
    allowed = (s_at <= t_at) & (seg_s == seg_t)
    q_copy.wait()
    go_copy.wait()

    kv_copy.wait_recv()
    kv = (kvs[mine] + kvr[...]).astype(BF16)
    kb, vb = kv[:, :HD], kv[:, HD:]

    gk = jnp.zeros((TOK, HD), F32)
    gv = jnp.zeros((TOK, HD), F32)
    for h in range(GH):
        qh = qv[:, h * HD:(h + 1) * HD]
        goh = gov[:, h * HD:(h + 1) * HD]
        st = jnp.where(allowed, dot(kb, qh, NT) * SCALE, -1e30)
        top = jnp.max(st, axis=0, keepdims=True)
        ex = jnp.where(allowed, jnp.exp(st - top), 0.0)
        pr = ex * (1.0 / jnp.sum(ex, axis=0, keepdims=True))
        low = pr.astype(BF16)
        plow_s[h] = low
        dp = dot(vb, goh, NT)
        inner = jnp.sum(pr * dp, axis=0, keepdims=True)
        ds = (pr * (dp - inner) * SCALE).astype(BF16)
        gv += dot(low, goh)
        gk += dot(ds, qh)
    G[mine] = jnp.concatenate([gk, gv], axis=1).astype(BF16)
    g_copy = remote(G.at[mine], G.at[mine], g_sem.at[0], g_sem.at[1], at(x, y, z, other))
    g_copy.start()
    wait_bytes(G.at[theirs], g_sem.at[1])

    def partial(p, i):
        if p == 0:
            lhs = XT[i].reshape(BLK, 2 * TOK)
        else:
            lhs = XT.reshape(NZ * 2, NY, 32, 2 * TOK)[:, i].reshape(BLK, 2 * TOK)
        return dot(lhs, G[:, p * HD:(p + 1) * HD])

    H = BLK // 2

    def rs_copy(p, d, s, sub):
        step = 1 - 2 * d
        return remote(
            SB.at[p, d, s - 1, sub], RB.at[p, d, s - 1, sub],
            rs_send.at[p, d, s - 1, sub], rs_recv.at[p, d, s - 1, sub], neighbour(p, step),
        )

    def grad_tokens(zz):
        wz = jnp.concatenate([W[0, zz].reshape(BLK, HD), W[1, zz].reshape(BLK, HD)], axis=1)
        GT[zz] = dot(G[...], wz, NT).astype(BF16)
        pltpu.make_async_copy(GT.at[zz, mine], gtok.at[:, cols(zz, c)], gt_sem.at[0]).start()
        remote(GT.at[zz, theirs], gtok.at[:, cols(zz, c)], gt_sem.at[1], gt_sem.at[2], at(x, y, z, other)).start()

    def attend_out(h):
        attn[:, h * HD:(h + 1) * HD] = dot(plow_s[h], vb, TN).astype(BF16)

    for p in range(2):
        pos, n = ring(p)
        part = partial(p, (pos + 4) % n).astype(BF16)
        for d in range(2):
            SB[p, d, 0, d] = part[d * H:(d + 1) * H]
            rs_copy(p, d, 1, d).start()
    for s in range(2, 5):
        parts = {}
        for p in range(2):
            pos, n = ring(p)
            for d in range(2):
                step = 1 - 2 * d
                parts[p, d] = partial(p, (pos + step * (5 - s) + n) % n)
                if s == 2:
                    sub = 1 - d
                    SB[p, d, s - 1, sub] = parts[p, d][sub * H:(sub + 1) * H].astype(BF16)
                    rs_copy(p, d, s, sub).start()
        for p in range(2):
            for d in range(2):
                for sub in ((d,) if s == 2 else (d, 1 - d)):
                    rs_copy(p, d, s - 1, sub).wait_recv()
                    add = parts[p, d][sub * H:(sub + 1) * H] + RB[p, d, s - 2, sub].astype(F32)
                    SB[p, d, s - 1, sub] = add.astype(BF16)
                    rs_copy(p, d, s, sub).start()
        if s == 2:
            for h in range(GH):
                attend_out(h)
        else:
            for zz in range((s - 3) * 4, (s - 2) * 4):
                grad_tokens(zz)

    for p in range(2):
        pos, n = ring(p)
        own = partial(p, pos)
        for sub in range(2):
            total = own[sub * H:(sub + 1) * H]
            for d in range(2):
                rs_copy(p, d, 4, sub).wait_recv()
                total += RB[p, d, 3, sub].astype(F32)
            if p == 0:
                YS[0, sub] = total.astype(BF16).reshape(NY, 32, HD)
            else:
                YS[1, :, pl.ds(sub * 4, 4)] = total.astype(BF16).reshape(4, 2, 32, HD).transpose(1, 0, 2, 3)
        for k in range(1, 8):
            j = (((y if p == 0 else z)) + k) % 8
            target = at(x, j, z, c) if p == 0 else at(x, y, j, c)
            me = y if p == 0 else z
            remote(YS.at[p, :, j], YR.at[p, :, me], rs_d_send.at[p], rs_d_recv.at[p], target).start()
    for p in range(2):
        me = y if p == 0 else z
        YR[p, :, me] = YS[p, :, me]
        wait_bytes(YR.at[p, :, pl.ds(0, 7)], rs_d_recv.at[p])
        total = jnp.sum(YR[p].astype(F32), axis=1)
        XS[p] = total.astype(BF16)
        for k in range(2):
            for cc in range(2):
                xx = c * 2 + k
                src = XS.at[p, k, pl.ds(cc * 16, 16)]
                dst = XR.at[p, x]

                is_me = (xx == x) & (c == cc)

                @pl.when(is_me)
                def _():
                    pltpu.make_async_copy(src, dst, rs_x_recv.at[p]).start()

                @pl.when(jnp.logical_not(is_me))
                def _():
                    remote(src, dst, rs_x_send.at[p, k, cc], rs_x_recv.at[p], at(xx, y, z, cc)).start()
    for p in range(2):
        wait_bytes(XR.at[p], rs_x_recv.at[p])
        gw[:, p * HD:(p + 1) * HD] = jnp.sum(XR[p].astype(F32), axis=0)

    wait_bytes(gtok.at[:, pl.ds(0, HALF)], gt_sem.at[0])
    wait_bytes(gtok.at[:, pl.ds(0, HALF)], gt_sem.at[1])
    wait_bytes(gtok.at[:, pl.ds(0, HALF)], gt_sem.at[2])
    for p in range(2):
        for k, xx in x_targets():
            cp = remote(sh.at[p], sh.at[p], ag_x_send.at[p, k], ag_x_recv.at[p], at(xx, y, z, home))
            if k == 0:
                @pl.when(home != c)
                def _():
                    cp.wait_send()
            else:
                cp.wait_send()
        wait_bytes(W.at[p, pl.ds(0, 7), :, 0], ag_d_send.at[p])
        wait_bytes(YR.at[p, :, pl.ds(0, 7)], rs_d_send.at[p])
        for d in range(2):
            for s in range(1, 5):
                for sub in range(2):
                    if s < 4 or sub == d:
                        ag_copy(p, d, s, sub).wait_send()
                    if s > 1 or sub == d:
                        rs_copy(p, d, s, sub).wait_send()
        for k in range(2):
            for cc in range(2):
                xx = c * 2 + k
                is_me = (xx == x) & (c == cc)

                @pl.when(jnp.logical_not(is_me))
                def _():
                    remote(XS.at[p, k, pl.ds(cc * 16, 16)], XR.at[p, x], rs_x_send.at[p, k, cc], rs_x_recv.at[p], at(xx, y, z, cc)).wait_send()
    wait_bytes(X.at[:, mine], tok_sem.at[0])
    kv_copy.wait_send()
    g_copy.wait_send()


def shards(tokens, queries, grad_out, seg_ids, w_values, w_scales):
    vmem = pl.BlockSpec(memory_space=pltpu.VMEM)
    hbm = pl.BlockSpec(memory_space=pl.ANY)
    dma = pltpu.SemaphoreType.DMA
    return tuple(pl.pallas_call(
        kernel,
        out_shape=(
            jax.ShapeDtypeStruct((TOK, GH * HD), BF16),
            jax.ShapeDtypeStruct((TOK, D), BF16),
            jax.ShapeDtypeStruct((16, 2 * HD), F32),
        ),
        in_specs=[hbm, hbm, hbm, vmem, vmem, vmem],
        out_specs=(vmem, hbm, vmem),
        scratch_shapes=[
            pltpu.VMEM((NZ, 2 * TOK, BLK), BF16),
            pltpu.VMEM((NZ, BLK, 2 * TOK), BF16),
            pltpu.VMEM((2, NZ, 2, NY, 32, HD), BF16),
            pltpu.VMEM((NZ, 2 * TOK, BLK), BF16),
            pltpu.VMEM((TOK, GH * HD), BF16),
            pltpu.VMEM((TOK, GH * HD), BF16),
            pltpu.VMEM((GH, TOK, TOK), BF16),
            pltpu.VMEM((2, 16, HD), BF16),
            pltpu.VMEM((2 * TOK, 2 * HD), F32),
            pltpu.VMEM((TOK, 2 * HD), F32),
            pltpu.VMEM((2 * TOK, 2 * HD), BF16),
            pltpu.VMEM((2, 2, 4, 2, BLK // 2, HD), BF16),
            pltpu.VMEM((2, 2, 4, 2, BLK // 2, HD), BF16),
            pltpu.VMEM((2, 2, 8, 32, HD), BF16),
            pltpu.VMEM((2, 2, 8, 32, HD), BF16),
            pltpu.VMEM((2, 2, 32, HD), BF16),
            pltpu.VMEM((2, NX, 16, HD), BF16),
            dma((3,)), dma((2,)), dma((2, NX)), dma((2,)), dma((2,)), dma((2,)),
            dma((2, 2, 4, 2)), dma((2, 2, 4, 2)),
            dma((2,)), dma((2,)), dma((3,)),
            dma((2, 2, 4, 2)), dma((2, 2, 4, 2)),
            dma((2,)), dma((2,)), dma((2, 2, 2)), dma((2,)),
        ],
        compiler_params=pltpu.CompilerParams(
            collective_id=0, has_side_effects=True, vmem_limit_bytes=48 * 2**20
        ),
        cost_estimate=pl.CostEstimate(flops=2 * 10**9, bytes_accessed=5 * 2**20, transcendentals=131072),
        name="layer",
    )(tokens, queries, grad_out, seg_ids, w_values, w_scales.reshape(1, 4)))


def solution(mesh):
    spec = P(("node", "dev"), None)
    return jax.shard_map(
        shards,
        mesh=mesh,
        in_specs=(spec, spec, spec, spec, spec, P()),
        out_specs=(spec, spec, spec),
        check_vma=False,
    )
```

time: 480 us -> 85.9 us (0.18)
  waiting for transfers between devices: 328 us -> 0 us
  blocking collectives: 100 us -> 0 us
  Pallas kernels: 0 us -> 76.8 us
  matrix products: 14 us -> 0 us
  between operations: 14.1 us -> 0.65 us
  other arithmetic: 6.44 us -> 0 us
    reduce_scatter x1 -> x0, waiting for transfers between devices: 202 us -> none  [shards(): lax.psum_scatter(node_group.astype(jnp.float32).astype(jnp.bfloat16), 'no...]
    all_gather x1 -> x0, waiting for transfers between devices: 125 us -> none  [shards(): full_values = lax.all_gather(w_values, ('node', 'dev'), axis=0, tiled=True)]
    all_to_all x1 -> x0, blocking collectives: 100 us -> none  [shards(): lax.all_to_all(blocks, 'dev', split_axis=1, concat_axis=1, tiled=True)]
    pallas_call x0 -> x1, Pallas kernels: none -> 76.8 us  [shards(): pl.pallas_call(kernel, out_shape=(jax.ShapeDtypeStruct((TOK, GH * HD), BF...]
    dot_general x8 -> x0, matrix products: 14 us -> none  [the longest x1 4.7 us: shards(): lax.dot_general(grad_kv, weight, (((1,), (1,)), ((), ())), preferred_elem...]
    unnamed x5 -> x15, local copies, waits for them, and re-layouts: 0.94 us -> 8.12 us
    convert_element_type x1 -> x0, local copies, waits for them, and re-layouts: 6.35 us -> none  [shards(): partial_value = lax.dot_general(tokens, grad_kv, (((0,), (0,)), ((), ()))...]
  transfers between devices with their start and end apart: 2 -> 0, of which waited for: 2 -> 0; matrix products, arithmetic and copies ran while one was open for 2% -> 0% of each run, Pallas kernels for 0% -> 0%
where the time goes in v1:
time: 85.9 us; the launch traced here: 85.6 us
  Pallas kernels  76.8 us (89%)
  local copies, waits for them, and re-layouts  8.12 us (9%)
    pallas_call x1, Pallas kernels, shards(): pl.pallas_call(kernel, out_shape=(jax.ShapeDtypeStruct((TOK, GH * HD), BF...  76.8 us
    unnamed x15, local copies, waits for them, and re-layouts  8.12 us

profile of v1, /device:TPU:1, one launch (start us, length us, event | category | flops | bytes accessed | tf_op | source)
XLA Modules:
  0.0 85.6 jit_solution(12178130813415452614)
XLA Ops:
  0.6 0.0 copy-start
  0.6 1.6 %copy-done = bf16[128,8192]{1,0:T(8,128)(2,1)S(1)} copy-done((bf16[128,8192]{1,0:T(8,128)(2,1)S(1)}, bf16[128,8192]{1,0:T(8,128)(2,1)}, u32[]{:S(2)}) %copy-start) | copy-done | bytes 2097176
  2.2 0.0 copy-start.1
  2.2 0.9 %copy-done.1 = bf16[128,1024]{1,0:T(8,128)(2,1)S(1)} copy-done((bf16[128,1024]{1,0:T(8,128)(2,1)S(1)}, bf16[128,1024]{1,0:T(8,128)(2,1)}, u32[]{:S(2)}) %copy-start.1) | copy-done | bytes 262168
  3.2 0.0 copy-start.2
  3.2 0.9 %copy-done.2 = bf16[128,1024]{1,0:T(8,128)(2,1)S(1)} copy-done((bf16[128,1024]{1,0:T(8,128)(2,1)S(1)}, bf16[128,1024]{1,0:T(8,128)(2,1)}, u32[]{:S(2)}) %copy-start.2) | copy-done | bytes 262168
  4.1 0.0 copy-start.3
  4.1 0.7 copy-done.3
  4.8 0.0 copy-start.4
  4.8 0.7 copy-done.4
  5.5 0.0 copy-start.5
  5.5 0.7 copy-done.5
  6.1 76.8 %layer.1 = (bf16[128,1024]{1,0:T(8,128)(2,1)S(1)}, bf16[128,8192]{1,0:T(8,128)(2,1)S(1)}, f32[16,256]{1,0:T(8,128)S(1)}) custom-call(bf16[128,8192]{1,0:T(8,128)(2,1)S(1)} %copy-done, bf16[128,1024]{1,0:T(8,128)(2,1)S(1)} %copy-done.1, bf16[128,1024]{1,0:T(8,128)(2,1)S(1)} %copy-done.2, s32[1,128]{1,0:T(1,128)S(1)} %copy-done.4, ...), custom_call_target="tpu_custom_call" | custom-call | flops 2000000000 | bytes 5242880 | tf_op jit(solution)/shard_map/layer/pallas_call | solution.py:344
  83.0 0.7 copy.12
  83.7 1.3 %copy.13 = bf16[128,8192]{1,0:T(8,128)(2,1)} copy(bf16[128,8192]{1,0:T(8,128)(2,1)S(1)} %get-tuple-element.7) | data formatting | bytes 4194304
  85.0 0.6 copy.14
Async XLA Ops:
  0.6 1.6 %copy-start = (bf16[128,8192]{1,0:T(8,128)(2,1)S(1)}, bf16[128,8192]{1,0:T(8,128)(2,1)}, u32[]{:S(2)}) copy-start(bf16[128,8192]{1,0:T(8,128)(2,1)} %tok.1) | copy-start | bytes 6291460
  2.2 0.9 %copy-start.1 = (bf16[128,1024]{1,0:T(8,128)(2,1)S(1)}, bf16[128,1024]{1,0:T(8,128)(2,1)}, u32[]{:S(2)}) copy-start(bf16[128,1024]{1,0:T(8,128)(2,1)} %q_hbm.1) | copy-start | bytes 786436
  3.2 0.9 %copy-start.2 = (bf16[128,1024]{1,0:T(8,128)(2,1)S(1)}, bf16[128,1024]{1,0:T(8,128)(2,1)}, u32[]{:S(2)}) copy-start(bf16[128,1024]{1,0:T(8,128)(2,1)} %go_hbm.1) | copy-start | bytes 786436
  4.1 0.7 copy-start.3
  4.8 0.7 copy-start.4
  5.5 0.7 copy-start.5

commit v2 on v0

v2 whole, which is shorter than its diff:
```python
import jax
import jax.numpy as jnp
from jax import lax
from jax.experimental import pallas as pl
from jax.experimental.pallas import tpu as pltpu
from jax.sharding import PartitionSpec as P

HD = 128
GH = 8
NX, NY, NZ = 4, 8, 8
TOK = 128
D = 8192
HALF = D // 2
BLK = HALF // NZ
SCALE = HD ** (-0.5)
MESH = pl.DeviceIdType.MESH
F32, BF16 = jnp.float32, jnp.bfloat16
NT = (((1,), (1,)), ((), ()))
TN = (((0,), (0,)), ((), ()))
NN = (((1,), (0,)), ((), ()))
K, V = 0, 1
FAR_X = (2, 1, 3, 0)
FAR = (4, 3, 5, 2, 6, 1, 7, 0)


def dot(a, b, dims=NN):
    return lax.dot_general(a, b, dims, preferred_element_type=F32)


def wait_bytes(ref, sem):
    pltpu.make_async_copy(ref, ref, sem).wait()


def kernel(
    tok, q_hbm, go_hbm, seg, w, scales,
    attn, gtok, gw,
    X, XT, W, GT, qv, gov, prob_s, low_s, sh, kvs, kvr, G, SB, RB, YS, XR,
    l_sem, tok_sem, ag_d_send, ag_d_recv, ag_send, ag_recv,
    kv_sem, g_sem, gt_sem, rs_send, rs_recv, rs_d_send, rs_d_recv,
):
    node, dev = lax.axis_index("node"), lax.axis_index("dev")
    z, x = node // NX, node % NX
    y, c = dev // 2, dev % 2
    other = 1 - c
    home = x // 2

    def at(x, y, z, c):
        return {"node": z * NX + x, "dev": y * 2 + c}

    def remote(src, dst, ss, rs, target):
        return pltpu.make_async_remote_copy(
            src_ref=src, dst_ref=dst, send_sem=ss, recv_sem=rs, device_id=target, device_id_type=MESH
        )

    def cols(zz, core):
        return pl.ds(pl.multiple_of(zz * 2 * BLK + core * BLK, BLK), BLK)

    mine = pl.ds(pl.multiple_of(c * TOK, TOK), TOK)
    theirs = pl.ds(pl.multiple_of(other * TOK, TOK), TOK)

    for zz in range(NZ):
        pltpu.make_async_copy(tok.at[:, cols(zz, c)], X.at[zz, mine], l_sem.at[0]).start()
    q_copy = pltpu.make_async_copy(q_hbm, qv, l_sem.at[1])
    go_copy = pltpu.make_async_copy(go_hbm, gov, l_sem.at[2])
    q_copy.start()
    go_copy.start()

    bar = pltpu.get_barrier_semaphore()

    def greet(device):
        pl.semaphore_signal(bar, inc=1, device_id=device, device_id_type=MESH)

    def gather_target(kx, kk):
        return at((x + kx) % NX, (y + kk * other) % NY, (z + kk * c) % NZ, home)

    def owner(r, xh, kk):
        return at(c * 2 + xh, (y + kk) % NY if r == 0 else y, z if r == 0 else (z + kk) % NZ, r)

    for kk in FAR:
        for kx in FAR_X:
            if kk == 0 and kx == 0:
                @pl.when(home != c)
                def _():
                    greet(gather_target(0, 0))
            else:
                greet(gather_target(kx, kk))
        for r in range(2):
            for xh in range(2):
                if kk == 0:
                    @pl.when(jnp.logical_not((r == c) & (c * 2 + xh == x)))
                    def _():
                        greet(owner(r, xh, 0))
                else:
                    greet(owner(r, xh, kk))
    for step in (1, 7):
        greet(at(x, (y + step) % NY, z, c))
        greet(at(x, y, (z + step) % NZ, c))
    greet(at(x, y, z, other))

    pick = lax.broadcasted_iota(jnp.int32, (1, 4), 1) == z // 2
    scale = jnp.sum(jnp.where(pick, scales[...].astype(F32), 0.0), axis=1, keepdims=True)
    scaled = (w[...].astype(F32) * scale).astype(BF16)
    sh[K] = scaled[:, :HD]
    sh[V] = scaled[:, HD:]

    @pl.when(home == c)
    def _():
        pl.semaphore_wait(bar, 67)

    @pl.when(home != c)
    def _():
        pl.semaphore_wait(bar, 69)

    place = W.at[:, z * 2 + x % 2, y, c]
    for kk in FAR:
        for kx in FAR_X:
            cp = remote(sh, place, ag_d_send, ag_d_recv.at[c], gather_target(kx, kk))
            if kk == 0 and kx == 0:
                @pl.when(home != c)
                def _():
                    cp.start()

                @pl.when(home == c)
                def _():
                    pltpu.make_async_copy(sh, place, ag_d_recv.at[c]).start()
            else:
                cp.start()

    for zz in range(NZ):
        remote(tok.at[:, cols(zz, other)], X.at[zz, mine], tok_sem.at[0], tok_sem.at[1], at(x, y, z, other)).start()

    wait_bytes(X.at[:, mine], l_sem.at[0])
    wait_bytes(X.at[:, theirs], tok_sem.at[1])

    def turn(zz):
        XT[pl.ds(2 * zz, 2)] = X[zz].T.reshape(2, NY, 2, 16, 2 * TOK)

    for zz in range(4):
        turn(zz)

    def piece(p, r, i, sub):
        if r == 0:
            return W.at[p, i * 2 + sub, :, 0]
        return W.at[p, pl.ds(sub * NZ, NZ), i, 1]

    def neighbour(r, step):
        if r == 0:
            return at(x, y, (z + step + NZ) % NZ, c)
        return at(x, (y + step + NY) % NY, z, c)

    pos = (z, y)

    def ag_copy(p, r, d, s, sub):
        step = 1 - 2 * d
        part = piece(p, r, (pos[r] - step * (s - 1) + 8) % 8, sub)
        return remote(part, part, ag_send.at[p], ag_recv.at[p, r, d, s - 1, sub], neighbour(r, step))

    def ag_arrival(p, r, d, s, sub):
        step = 1 - 2 * d
        wait_bytes(piece(p, r, (pos[r] - step * s + 8) % 8, sub), ag_recv.at[p, r, d, s - 1, sub])

    wait_bytes(W.at[:, pl.ds(z * 2, 2), :, 0], ag_d_recv.at[0])
    wait_bytes(W.at[:, :, y, 1], ag_d_recv.at[1])
    streams = ((K, 0), (K, 1), (V, 0), (V, 1))
    for n, (p, sub) in enumerate(streams):
        for r in range(2):
            for d in range(2):
                ag_copy(p, r, d, 1, sub).start()
        turn(4 + n)
    for s in range(2, 5):
        for p, sub in streams:
            for r in range(2):
                for d in range(2):
                    ag_arrival(p, r, d, s - 1, sub)
                    if s < 4 or sub == d:
                        ag_copy(p, r, d, s, sub).start()

    def kv_copy(p):
        return remote(kvs.at[p, theirs], kvr.at[p], kv_sem.at[p], kv_sem.at[2 + p], at(x, y, z, other))

    def rows(p, zz):
        return W[p, pl.ds(2 * zz, 2)].reshape(BLK, HD)

    for p in range(2):
        for r in range(2):
            for sub in range(2):
                ag_arrival(p, r, sub, 4, sub)
        acc = jnp.zeros((2 * TOK, HD), F32)
        for zz in range(NZ):
            acc += dot(X[zz], rows(p, zz))
        kvs[p] = acc
        kv_copy(p).start()

    seg_t = jnp.broadcast_to(seg[...].astype(F32), (TOK, TOK))
    seg_s = seg_t.T
    s_at = lax.broadcasted_iota(jnp.int32, (TOK, TOK), 0)
    t_at = lax.broadcasted_iota(jnp.int32, (TOK, TOK), 1)
    allowed = (s_at <= t_at) & (seg_s == seg_t)
    q_copy.wait()
    go_copy.wait()

    def head(ref, h):
        return ref[:, h * HD:(h + 1) * HD]

    def g_copy(p):
        return remote(G.at[p, mine], G.at[p, mine], g_sem.at[p], g_sem.at[2 + p], at(x, y, z, other))

    kv_copy(K).wait_recv()
    kb = (kvs[K, mine] + kvr[K]).astype(BF16)
    gv = jnp.zeros((TOK, HD), F32)
    for h in range(GH):
        st = jnp.where(allowed, dot(kb, head(qv, h), NT) * SCALE, -1e30)
        top = jnp.max(st, axis=0, keepdims=True)
        ex = jnp.where(allowed, jnp.exp(st - top), 0.0)
        pr = ex * (1.0 / jnp.sum(ex, axis=0, keepdims=True))
        low = pr.astype(BF16)
        prob_s[h] = pr
        low_s[h] = low
        gv += dot(low, head(gov, h))
    G[V, mine] = gv.astype(BF16)
    g_copy(V).start()

    kv_copy(V).wait_recv()
    vb = (kvs[V, mine] + kvr[V]).astype(BF16)
    gk = jnp.zeros((TOK, HD), F32)
    for h in range(GH):
        pr = prob_s[h]
        dp = dot(vb, head(gov, h), NT)
        inner = jnp.sum(pr * dp, axis=0, keepdims=True)
        ds = (pr * (dp - inner) * SCALE).astype(BF16)
        gk += dot(ds, head(qv, h))
    G[K, mine] = gk.astype(BF16)
    g_copy(K).start()

    def partial(p, r, i):
        if r == 0:
            lhs = XT[pl.ds(2 * i, 2), :, 0]
        else:
            lhs = XT[:, i, 1]
        return dot(lhs.reshape(2 * TOK, 2 * TOK), G[p])

    def rs_copy(p, r, d, s, sub):
        return remote(
            SB.at[p, r, d, s - 1, sub], RB.at[p, r, d, s - 1, sub],
            rs_send.at[p], rs_recv.at[p, r, d, s - 1, sub], neighbour(r, 1 - 2 * d),
        )

    def grad_tokens(zz):
        wz = jnp.concatenate([rows(K, zz), rows(V, zz)], axis=1)
        g = jnp.concatenate([G[K], G[V]], axis=1)
        GT[zz] = dot(g, wz, NT).astype(BF16)
        pltpu.make_async_copy(GT.at[zz, mine], gtok.at[:, cols(zz, c)], gt_sem.at[0]).start()
        remote(GT.at[zz, theirs], gtok.at[:, cols(zz, c)], gt_sem.at[1], gt_sem.at[2], at(x, y, z, other)).start()

    def attend_out(h):
        attn[:, h * HD:(h + 1) * HD] = dot(low_s[h], vb, TN).astype(BF16)

    H = TOK
    for p in (V, K):
        wait_bytes(G.at[p, theirs], g_sem.at[2 + p])
        for r in range(2):
            part = partial(p, r, (pos[r] + 4) % 8).astype(BF16)
            for d in range(2):
                SB[p, r, d, 0, d] = part[d * H:(d + 1) * H]
                rs_copy(p, r, d, 1, d).start()
    for s in range(2, 5):
        for p in (V, K):
            parts = {}
            for r in range(2):
                for d in range(2):
                    step = 1 - 2 * d
                    parts[r, d] = partial(p, r, (pos[r] + step * (5 - s) + 8) % 8)
                    if s == 2:
                        sub = 1 - d
                        SB[p, r, d, s - 1, sub] = parts[r, d][sub * H:(sub + 1) * H].astype(BF16)
                        rs_copy(p, r, d, s, sub).start()
            for sub in range(2):
                for r in range(2):
                    for d in range(2):
                        if s == 2 and sub != d:
                            continue
                        rs_copy(p, r, d, s - 1, sub).wait_recv()
                        add = parts[r, d][sub * H:(sub + 1) * H] + RB[p, r, d, s - 2, sub].astype(F32)
                        SB[p, r, d, s - 1, sub] = add.astype(BF16)
                        rs_copy(p, r, d, s, sub).start()
            half = 0 if p == V else 1
            if s == 2:
                for h in range(half * 4, half * 4 + 4):
                    attend_out(h)
            else:
                for zz in range((s - 3) * 4 + half * 2, (s - 3) * 4 + half * 2 + 2):
                    grad_tokens(zz)

    for p in (V, K):
        for r in range(2):
            own = partial(p, r, pos[r])
            for sub in range(2):
                total = own[sub * H:(sub + 1) * H]
                for d in range(2):
                    rs_copy(p, r, d, 4, sub).wait_recv()
                    total += RB[p, r, d, 3, sub].astype(F32)
                YS[r, pl.ds(sub * 8, 8), p] = total.astype(BF16).reshape(8, 16, HD)
    for kk in FAR:
        for r in range(2):
            for xh in range(2):
                if r == 0:
                    src = YS.at[0, xh * 8 + (y + kk) % NY]
                    dst = XR.at[x * 8 + y]
                else:
                    src = YS.at[1, (z + kk) % NZ * 2 + xh]
                    dst = XR.at[x * 8 + z]
                cp = remote(src, dst, rs_d_send, rs_d_recv, owner(r, xh, kk))
                if kk == 0:
                    is_me = (r == c) & (c * 2 + xh == x)

                    @pl.when(jnp.logical_not(is_me))
                    def _():
                        cp.start()

                    @pl.when(is_me)
                    def _():
                        pltpu.make_async_copy(src, dst, rs_d_recv).start()
                else:
                    cp.start()

    for k in range(3):
        wait_bytes(gtok.at[:, pl.ds(0, HALF)], gt_sem.at[k])
    for p in range(2):
        wait_bytes(W.at[p, pl.ds(0, 14)], ag_send.at[p])
        wait_bytes(W.at[p, pl.ds(0, 14)], rs_send.at[p])
        kv_copy(p).wait_send()
        g_copy(p).wait_send()
    wait_bytes(X.at[:, mine], tok_sem.at[0])

    @pl.when(home == c)
    def _():
        wait_bytes(XR.at[pl.ds(0, 31)], ag_d_send)

    @pl.when(home != c)
    def _():
        wait_bytes(XR, ag_d_send)

    wait_bytes(XR, rs_d_recv)
    for p in range(2):
        gw[:, p * HD:(p + 1) * HD] = jnp.sum(XR[:, p].astype(F32), axis=0)

    @pl.when(home == c)
    def _():
        wait_bytes(XR.at[pl.ds(0, 31)], rs_d_send)

    @pl.when(home != c)
    def _():
        wait_bytes(XR, rs_d_send)


def shards(tokens, queries, grad_out, seg_ids, w_values, w_scales):
    vmem = pl.BlockSpec(memory_space=pltpu.VMEM)
    hbm = pl.BlockSpec(memory_space=pl.ANY)
    dma = pltpu.SemaphoreType.DMA
    return tuple(pl.pallas_call(
        kernel,
        out_shape=(
            jax.ShapeDtypeStruct((TOK, GH * HD), BF16),
            jax.ShapeDtypeStruct((TOK, D), BF16),
            jax.ShapeDtypeStruct((16, 2 * HD), F32),
        ),
        in_specs=[hbm, hbm, hbm, vmem, vmem, vmem],
        out_specs=(vmem, hbm, vmem),
        scratch_shapes=[
            pltpu.VMEM((NZ, 2 * TOK, BLK), BF16),
            pltpu.VMEM((2 * NZ, NY, 2, 16, 2 * TOK), BF16),
            pltpu.VMEM((2, 2 * NZ, NY, 2, 16, HD), BF16),
            pltpu.VMEM((NZ, 2 * TOK, BLK), BF16),
            pltpu.VMEM((TOK, GH * HD), BF16),
            pltpu.VMEM((TOK, GH * HD), BF16),
            pltpu.VMEM((GH, TOK, TOK), F32),
            pltpu.VMEM((GH, TOK, TOK), BF16),
            pltpu.VMEM((2, 16, HD), BF16),
            pltpu.VMEM((2, 2 * TOK, HD), F32),
            pltpu.VMEM((2, TOK, HD), F32),
            pltpu.VMEM((2, 2 * TOK, HD), BF16),
            pltpu.VMEM((2, 2, 2, 4, 2, TOK, HD), BF16),
            pltpu.VMEM((2, 2, 2, 4, 2, TOK, HD), BF16),
            pltpu.VMEM((2, 16, 2, 16, HD), BF16),
            pltpu.VMEM((32, 2, 16, HD), BF16),
            dma((3,)), dma((2,)), dma, dma((2,)), dma((2,)), dma((2, 2, 2, 4, 2)),
            dma((4,)), dma((4,)), dma((3,)), dma((2,)), dma((2, 2, 2, 4, 2)), dma, dma,
        ],
        compiler_params=pltpu.CompilerParams(
            collective_id=0, has_side_effects=True, vmem_limit_bytes=60 * 2**20
        ),
        cost_estimate=pl.CostEstimate(flops=2 * 10**9, bytes_accessed=5 * 2**20, transcendentals=131072),
        name="layer",
    )(tokens, queries, grad_out, seg_ids, w_values, w_scales.reshape(1, 4)))


def solution(mesh):
    spec = P(("node", "dev"), None)
    return jax.shard_map(
        shards,
        mesh=mesh,
        in_specs=(spec, spec, spec, spec, spec, P()),
        out_specs=(spec, spec, spec),
        check_vma=False,
    )
```

time: 480 us -> 74.7 us (0.16)
  waiting for transfers between devices: 328 us -> 0 us
  blocking collectives: 100 us -> 0 us
  Pallas kernels: 0 us -> 68.4 us
  matrix products: 14 us -> 0 us
  between operations: 14.1 us -> 0.64 us
  local copies, waits for them, and re-layouts: 12.2 us -> 5.39 us
  other arithmetic: 6.44 us -> 0 us
    reduce_scatter x1 -> x0, waiting for transfers between devices: 202 us -> none  [shards(): lax.psum_scatter(node_group.astype(jnp.float32).astype(jnp.bfloat16), 'no...]
    all_gather x1 -> x0, waiting for transfers between devices: 125 us -> none  [shards(): full_values = lax.all_gather(w_values, ('node', 'dev'), axis=0, tiled=True)]
    all_to_all x1 -> x0, blocking collectives: 100 us -> none  [shards(): lax.all_to_all(blocks, 'dev', split_axis=1, concat_axis=1, tiled=True)]
    pallas_call x0 -> x1, Pallas kernels: none -> 68.4 us  [shards(): pl.pallas_call(kernel, out_shape=(jax.ShapeDtypeStruct((TOK, GH * HD), BF...]
    dot_general x8 -> x0, matrix products: 14 us -> none  [the longest x1 4.7 us: shards(): lax.dot_general(grad_kv, weight, (((1,), (1,)), ((), ())), preferred_elem...]
    convert_element_type x1 -> x0, local copies, waits for them, and re-layouts: 6.35 us -> none  [shards(): partial_value = lax.dot_general(tokens, grad_kv, (((0,), (0,)), ((), ()))...]
  transfers between devices with their start and end apart: 2 -> 0, of which waited for: 2 -> 0; matrix products, arithmetic and copies ran while one was open for 2% -> 0% of each run, Pallas kernels for 0% -> 0%
where the time goes in v2:
time: 74.7 us; the launch traced here: 74.4 us
  Pallas kernels  68.4 us (92%)
  local copies, waits for them, and re-layouts  5.39 us (7%)
    pallas_call x1, Pallas kernels, shards(): pl.pallas_call(kernel, out_shape=(jax.ShapeDtypeStruct((TOK, GH * HD), BF...  68.4 us
    unnamed x5, local copies, waits for them, and re-layouts  5.39 us

profile of v2, /device:TPU:1, one launch (start us, length us, event | category | flops | bytes accessed | tf_op | source)
XLA Modules:
  0.0 74.4 jit_solution(10560484105748434409)
XLA Ops:
  0.6 68.4 %layer.1 = (bf16[128,1024]{1,0:T(8,128)(2,1)}, bf16[128,8192]{1,0:T(8,128)(2,1)}, f32[16,256]{1,0:T(8,128)}) custom-call(bf16[128,8192]{1,0:T(8,128)(2,1)} %tok.1, bf16[128,1024]{1,0:T(8,128)(2,1)} %q_hbm.1, bf16[128,1024]{1,0:T(8,128)(2,1)} %go_hbm.1, s32[1,128]{1,0:T(1,128)} %seg.1, bf16[16,256]{1,0:T(8,128)(2,1)} %w.1, bf16[1,4]{1,0:T(2,128)(2,1)} %bitcast.1), custom_call_target="tpu_custom_call" | custom-call | flops 2000000000 | bytes 5242880 | tf_op jit(solution)/shard_map/layer/pallas_call | solution.py:360
  69.1 1.7 %copy.12 = bf16[128,1024]{1,0:T(8,128)(2,1)} copy(bf16[128,1024]{1,0:T(8,128)(2,1)} %get-tuple-element.6) | data formatting | bytes 524288
  70.7 0.0 copy-start
  70.7 3.1 %copy.13 = bf16[128,8192]{1,0:T(8,128)(2,1)} copy(bf16[128,8192]{1,0:T(8,128)(2,1)} %get-tuple-element.7) | data formatting | bytes 4194304
  73.8 0.0 copy-done
  73.8 0.6 copy.14
Async XLA Ops:
  70.7 3.1 %copy-start = (f32[16,256]{1,0:T(8,128)S(1)}, f32[16,256]{1,0:T(8,128)}, u32[]{:S(2)}) copy-start(f32[16,256]{1,0:T(8,128)} %get-tuple-element.8) | copy-start | bytes 49156

commit v3 on v2

--- a/solution.py
+++ b/solution.py
@@ -32,9 +32,9 @@
 
 
 def kernel(
-    tok, q_hbm, go_hbm, seg, w, scales,
+    tok, q_hbm, go_hbm, seg_hbm, w_hbm, scales_hbm,
     attn, gtok, gw,
-    X, XT, W, GT, qv, gov, prob_s, low_s, sh, kvs, kvr, G, SB, RB, YS, XR,
+    seg, w, scales, X, XT, W, GT, qv, gov, prob_s, low_s, sh, kvs, kvr, G, SB, RB, YS, XR,
     l_sem, tok_sem, ag_d_send, ag_d_recv, ag_send, ag_recv,
     kv_sem, g_sem, gt_sem, rs_send, rs_recv, rs_d_send, rs_d_recv,
 ):
@@ -57,13 +57,6 @@
 
     mine = pl.ds(pl.multiple_of(c * TOK, TOK), TOK)
     theirs = pl.ds(pl.multiple_of(other * TOK, TOK), TOK)
-
-    for zz in range(NZ):
-        pltpu.make_async_copy(tok.at[:, cols(zz, c)], X.at[zz, mine], l_sem.at[0]).start()
-    q_copy = pltpu.make_async_copy(q_hbm, qv, l_sem.at[1])
-    go_copy = pltpu.make_async_copy(go_hbm, gov, l_sem.at[2])
-    q_copy.start()
-    go_copy.start()
 
     bar = pltpu.get_barrier_semaphore()
 
@@ -97,6 +90,21 @@
         greet(at(x, y, (z + step) % NZ, c))
     greet(at(x, y, z, other))
 
+    small = [
+        pltpu.make_async_copy(src, dst, l_sem.at[3 + n])
+        for n, (src, dst) in enumerate(((w_hbm, w), (scales_hbm, scales), (seg_hbm, seg)))
+    ]
+    for copy in small:
+        copy.start()
+    for zz in range(NZ):
+        pltpu.make_async_copy(tok.at[:, cols(zz, c)], X.at[zz, mine], l_sem.at[0]).start()
+    q_copy = pltpu.make_async_copy(q_hbm, qv, l_sem.at[1])
+    go_copy = pltpu.make_async_copy(go_hbm, gov, l_sem.at[2])
+    q_copy.start()
+    go_copy.start()
+
+    small[0].wait()
+    small[1].wait()
     pick = lax.broadcasted_iota(jnp.int32, (1, 4), 1) == z // 2
     scale = jnp.sum(jnp.where(pick, scales[...].astype(F32), 0.0), axis=1, keepdims=True)
     scaled = (w[...].astype(F32) * scale).astype(BF16)
@@ -191,16 +199,18 @@
         kvs[p] = acc
         kv_copy(p).start()
 
+    small[2].wait()
     seg_t = jnp.broadcast_to(seg[...].astype(F32), (TOK, TOK))
     seg_s = seg_t.T
     s_at = lax.broadcasted_iota(jnp.int32, (TOK, TOK), 0)
     t_at = lax.broadcasted_iota(jnp.int32, (TOK, TOK), 1)
-    allowed = (s_at <= t_at) & (seg_s == seg_t)
+    one = jnp.where((s_at <= t_at) & (seg_s == seg_t), 1.0, 0.0)
+    allowed = jnp.concatenate([one, one], axis=1) > 0.5
     q_copy.wait()
     go_copy.wait()
 
-    def head(ref, h):
-        return ref[:, h * HD:(h + 1) * HD]
+    def pair(ref, h):
+        return jnp.concatenate([ref[:, h * HD:(h + 1) * HD], ref[:, (h + 1) * HD:(h + 2) * HD]], axis=0)
 
     def g_copy(p):
         return remote(G.at[p, mine], G.at[p, mine], g_sem.at[p], g_sem.at[2 + p], at(x, y, z, other))
@@ -208,27 +218,27 @@
     kv_copy(K).wait_recv()
     kb = (kvs[K, mine] + kvr[K]).astype(BF16)
     gv = jnp.zeros((TOK, HD), F32)
-    for h in range(GH):
-        st = jnp.where(allowed, dot(kb, head(qv, h), NT) * SCALE, -1e30)
+    for h in range(0, GH, 2):
+        st = jnp.where(allowed, dot(kb, pair(qv, h), NT) * SCALE, -1e30)
         top = jnp.max(st, axis=0, keepdims=True)
         ex = jnp.where(allowed, jnp.exp(st - top), 0.0)
         pr = ex * (1.0 / jnp.sum(ex, axis=0, keepdims=True))
         low = pr.astype(BF16)
-        prob_s[h] = pr
-        low_s[h] = low
-        gv += dot(low, head(gov, h))
+        prob_s[h // 2] = pr
+        low_s[h // 2] = low
+        gv += dot(low, pair(gov, h))
     G[V, mine] = gv.astype(BF16)
     g_copy(V).start()
 
     kv_copy(V).wait_recv()
     vb = (kvs[V, mine] + kvr[V]).astype(BF16)
     gk = jnp.zeros((TOK, HD), F32)
-    for h in range(GH):
-        pr = prob_s[h]
-        dp = dot(vb, head(gov, h), NT)
+    for h in range(0, GH, 2):
+        pr = prob_s[h // 2]
+        dp = dot(vb, pair(gov, h), NT)
         inner = jnp.sum(pr * dp, axis=0, keepdims=True)
         ds = (pr * (dp - inner) * SCALE).astype(BF16)
-        gk += dot(ds, head(qv, h))
+        gk += dot(ds, pair(qv, h))
     G[K, mine] = gk.astype(BF16)
     g_copy(K).start()
 
@@ -249,11 +259,11 @@
         wz = jnp.concatenate([rows(K, zz), rows(V, zz)], axis=1)
         g = jnp.concatenate([G[K], G[V]], axis=1)
         GT[zz] = dot(g, wz, NT).astype(BF16)
-        pltpu.make_async_copy(GT.at[zz, mine], gtok.at[:, cols(zz, c)], gt_sem.at[0]).start()
-        remote(GT.at[zz, theirs], gtok.at[:, cols(zz, c)], gt_sem.at[1], gt_sem.at[2], at(x, y, z, other)).start()
+        gtok[:, cols(zz, c)] = GT[zz, mine]
+        remote(GT.at[zz, theirs], gtok.at[:, cols(zz, c)], gt_sem.at[0], gt_sem.at[1], at(x, y, z, other)).start()
 
     def attend_out(h):
-        attn[:, h * HD:(h + 1) * HD] = dot(low_s[h], vb, TN).astype(BF16)
+        attn[:, h * HD:(h + 1) * HD] = dot(low_s[h // 2, :, h % 2 * TOK:(h % 2 + 1) * TOK], vb, TN).astype(BF16)
 
     H = TOK
     for p in (V, K):
@@ -323,7 +333,7 @@
                 else:
                     cp.start()
 
-    for k in range(3):
+    for k in range(2):
         wait_bytes(gtok.at[:, pl.ds(0, HALF)], gt_sem.at[k])
     for p in range(2):
         wait_bytes(W.at[p, pl.ds(0, 14)], ag_send.at[p])
@@ -353,28 +363,38 @@
         wait_bytes(XR, rs_d_send)
 
 
+OUTS = (((TOK, GH * HD), BF16), ((TOK, D), BF16), ((16, 2 * HD), F32))
+
+
+def write_out(*refs):
+    copies = [pltpu.make_async_copy(refs[i], refs[3 + i], refs[6].at[i]) for i in range(3)]
+    for copy in copies:
+        copy.start()
+    for copy in copies:
+        copy.wait()
+
+
 def shards(tokens, queries, grad_out, seg_ids, w_values, w_scales):
     vmem = pl.BlockSpec(memory_space=pltpu.VMEM)
-    hbm = pl.BlockSpec(memory_space=pl.ANY)
+    hbm = pl.BlockSpec(memory_space=pltpu.HBM)
     dma = pltpu.SemaphoreType.DMA
-    return tuple(pl.pallas_call(
+    inner = pl.pallas_call(
         kernel,
-        out_shape=(
-            jax.ShapeDtypeStruct((TOK, GH * HD), BF16),
-            jax.ShapeDtypeStruct((TOK, D), BF16),
-            jax.ShapeDtypeStruct((16, 2 * HD), F32),
-        ),
-        in_specs=[hbm, hbm, hbm, vmem, vmem, vmem],
-        out_specs=(vmem, hbm, vmem),
+        out_shape=tuple(pltpu.VMEM(shape, dtype) for shape, dtype in OUTS),
+        in_specs=[hbm] * 6,
+        out_specs=(vmem, vmem, vmem),
         scratch_shapes=[
+            pltpu.VMEM((1, TOK), jnp.int32),
+            pltpu.VMEM((16, 2 * HD), BF16),
+            pltpu.VMEM((1, 4), BF16),
             pltpu.VMEM((NZ, 2 * TOK, BLK), BF16),
             pltpu.VMEM((2 * NZ, NY, 2, 16, 2 * TOK), BF16),
             pltpu.VMEM((2, 2 * NZ, NY, 2, 16, HD), BF16),
             pltpu.VMEM((NZ, 2 * TOK, BLK), BF16),
             pltpu.VMEM((TOK, GH * HD), BF16),
             pltpu.VMEM((TOK, GH * HD), BF16),
-            pltpu.VMEM((GH, TOK, TOK), F32),
-            pltpu.VMEM((GH, TOK, TOK), BF16),
+            pltpu.VMEM((GH // 2, TOK, 2 * TOK), F32),
+            pltpu.VMEM((GH // 2, TOK, 2 * TOK), BF16),
             pltpu.VMEM((2, 16, HD), BF16),
             pltpu.VMEM((2, 2 * TOK, HD), F32),
             pltpu.VMEM((2, TOK, HD), F32),
@@ -383,15 +403,23 @@
             pltpu.VMEM((2, 2, 2, 4, 2, TOK, HD), BF16),
             pltpu.VMEM((2, 16, 2, 16, HD), BF16),
             pltpu.VMEM((32, 2, 16, HD), BF16),
-            dma((3,)), dma((2,)), dma, dma((2,)), dma((2,)), dma((2, 2, 2, 4, 2)),
-            dma((4,)), dma((4,)), dma((3,)), dma((2,)), dma((2, 2, 2, 4, 2)), dma, dma,
+            dma((6,)), dma((2,)), dma, dma((2,)), dma((2,)), dma((2, 2, 2, 4, 2)),
+            dma((4,)), dma((4,)), dma((2,)), dma((2,)), dma((2, 2, 2, 4, 2)), dma, dma,
         ],
         compiler_params=pltpu.CompilerParams(
             collective_id=0, has_side_effects=True, vmem_limit_bytes=60 * 2**20
         ),
         cost_estimate=pl.CostEstimate(flops=2 * 10**9, bytes_accessed=5 * 2**20, transcendentals=131072),
         name="layer",
-    )(tokens, queries, grad_out, seg_ids, w_values, w_scales.reshape(1, 4)))
+    )(tokens, queries, grad_out, seg_ids, w_values, w_scales.reshape(1, 4))
+    return tuple(pl.pallas_call(
+        write_out,
+        out_shape=tuple(jax.ShapeDtypeStruct(shape, dtype) for shape, dtype in OUTS),
+        in_specs=[vmem] * 3,
+        out_specs=(pl.BlockSpec(memory_space=pl.ANY),) * 3,
+        scratch_shapes=[dma((3,))],
+        name="write_out",
+    )(*inner))
 
 
 def solution(mesh):

time: 74.7 us -> 73.5 us (0.984)
  local copies, waits for them, and re-layouts: 5.39 us -> 2.64 us
  Pallas kernels: 68.4 us -> 70.1 us
    unnamed x5 -> x6, local copies, waits for them, and re-layouts: 5.39 us -> 2.64 us
    pallas_call x1 -> x2, Pallas kernels: 68.4 us -> 70.1 us  [the longest x1 67.1 us: shards(): pl.pallas_call(kernel, out_shape=tuple((pltpu.VMEM(shape, dtype) for shap...]
where the time goes in v3:
time: 73.5 us; the launch traced here: 73.4 us
  Pallas kernels  70.1 us (95%)
  local copies, waits for them, and re-layouts  2.64 us (4%)
    pallas_call x1, Pallas kernels, shards(): pl.pallas_call(kernel, out_shape=tuple((pltpu.VMEM(shape, dtype) for shap...  67.1 us
    pallas_call x1, Pallas kernels, shards(): pl.pallas_call(write_out, out_shape=tuple((jax.ShapeDtypeStruct(shape, dt...  3.02 us
    unnamed x6, local copies, waits for them, and re-layouts  2.64 us

profile of v3, /device:TPU:1, one launch (start us, length us, event | category | flops | bytes accessed | tf_op | source)
XLA Modules:
  0.0 73.4 jit_solution(18305163364861992370)
XLA Ops:
  0.6 67.1 %layer.1 = (bf16[128,1024]{1,0:T(8,128)(2,1)S(1)}, bf16[128,8192]{1,0:T(8,128)(2,1)S(1)}, f32[16,256]{1,0:T(8,128)S(1)}) custom-call(bf16[128,8192]{1,0:T(8,128)(2,1)} %tok.1, bf16[128,1024]{1,0:T(8,128)(2,1)} %q_hbm.1, bf16[128,1024]{1,0:T(8,128)(2,1)} %go_hbm.1, s32[1,128]{1,0:T(1,128)} %seg_hbm.1, bf16[16,256]{1,0:T(8,128)(2,1)} %w_hbm.1, ...), custom_call_target="tpu_custom_call" | custom-call | flops 2000000000 | bytes 5242880 | tf_op jit(solution)/shard_map/layer/pallas_call | solution.py:381
  67.7 0.0 copy-start
  67.7 1.3 %copy-done = bf16[128,8192]{1,0:T(8,128)(2,1)} copy-done((bf16[128,8192]{1,0:T(8,128)(2,1)}, bf16[128,8192]{1,0:T(8,128)(2,1)S(1)}, u32[]{:S(2)}) %copy-start) | copy-done | bytes 2097176
  69.0 0.0 copy-start.1
  69.0 0.7 copy-done.1
  69.8 0.0 copy-start.2
  69.8 0.6 copy-done.2
  70.4 3.0 %write_out.1 = (bf16[128,1024]{1,0:T(8,128)(2,1)}, bf16[128,8192]{1,0:T(8,128)(2,1)}, f32[16,256]{1,0:T(8,128)}) custom-call(bf16[128,1024]{1,0:T(8,128)(2,1)} %copy-done.1, bf16[128,8192]{1,0:T(8,128)(2,1)} %copy-done, f32[16,256]{1,0:T(8,128)} %copy-done.2), custom_call_target="tpu_custom_call" | custom-call | tf_op jit(solution)/shard_map/write_out/pallas_call | solution.py:415
Async XLA Ops:
  67.7 1.3 %copy-start = (bf16[128,8192]{1,0:T(8,128)(2,1)}, bf16[128,8192]{1,0:T(8,128)(2,1)S(1)}, u32[]{:S(2)}) copy-start(bf16[128,8192]{1,0:T(8,128)(2,1)S(1)} %get-tuple-element.7.refs_1_) | copy-start | bytes 6291460
  69.0 0.7 copy-start.1
  69.8 0.6 copy-start.2

commit v4 on v3

--- a/solution.py
+++ b/solution.py
@@ -85,7 +85,7 @@
                         greet(owner(r, xh, 0))
                 else:
                     greet(owner(r, xh, kk))
-    for step in (1, 7):
+    for step in (1, 2, 6, 7):
         greet(at(x, (y + step) % NY, z, c))
         greet(at(x, y, (z + step) % NZ, c))
     greet(at(x, y, z, other))
@@ -113,11 +113,11 @@
 
     @pl.when(home == c)
     def _():
-        pl.semaphore_wait(bar, 67)
+        pl.semaphore_wait(bar, 71)
 
     @pl.when(home != c)
     def _():
-        pl.semaphore_wait(bar, 69)
+        pl.semaphore_wait(bar, 73)
 
     place = W.at[:, z * 2 + x % 2, y, c]
     for kk in FAR:
@@ -158,30 +158,40 @@
 
     pos = (z, y)
 
-    def ag_copy(p, r, d, s, sub):
+    def ag_copy(p, r, d, k, places, sub):
         step = 1 - 2 * d
-        part = piece(p, r, (pos[r] - step * (s - 1) + 8) % 8, sub)
-        return remote(part, part, ag_send.at[p], ag_recv.at[p, r, d, s - 1, sub], neighbour(r, step))
-
-    def ag_arrival(p, r, d, s, sub):
-        step = 1 - 2 * d
-        wait_bytes(piece(p, r, (pos[r] - step * s + 8) % 8, sub), ag_recv.at[p, r, d, s - 1, sub])
+        part = piece(p, r, (pos[r] - step * k + 8) % 8, sub)
+        return remote(part, part, ag_send.at[p], ag_recv.at[p, r, d, k + places - 1, sub], neighbour(r, step * places))
+
+    def ag_arrival(p, r, d, k, sub):
+        wait_bytes(piece(p, r, (pos[r] - (1 - 2 * d) * k + 8) % 8, sub), ag_recv.at[p, r, d, k - 1, sub])
+
+    GOES = ({0: (2, 1), 2: (2, 1)}, {0: (1,), 1: (1,), 2: (2, 1)})
+
+    def ag_pass(p, k):
+        for sub in range(2):
+            for r in range(2):
+                for d in range(2):
+                    if k == 4 and sub != d:
+                        continue
+                    if k > 0:
+                        ag_arrival(p, r, d, k, sub)
+                    for places in GOES[p].get(k, ()):
+                        if k + places < 4 or sub == d:
+                            ag_copy(p, r, d, k, places, sub).start()
 
     wait_bytes(W.at[:, pl.ds(z * 2, 2), :, 0], ag_d_recv.at[0])
     wait_bytes(W.at[:, :, y, 1], ag_d_recv.at[1])
-    streams = ((K, 0), (K, 1), (V, 0), (V, 1))
-    for n, (p, sub) in enumerate(streams):
-        for r in range(2):
-            for d in range(2):
-                ag_copy(p, r, d, 1, sub).start()
-        turn(4 + n)
-    for s in range(2, 5):
-        for p, sub in streams:
-            for r in range(2):
-                for d in range(2):
-                    ag_arrival(p, r, d, s - 1, sub)
-                    if s < 4 or sub == d:
-                        ag_copy(p, r, d, s, sub).start()
+    ag_pass(K, 0)
+    ag_pass(V, 0)
+    for zz in range(4, 6):
+        turn(zz)
+    ag_pass(K, 2)
+    ag_pass(V, 1)
+    for zz in range(6, 8):
+        turn(zz)
+    ag_pass(K, 1)
+    ag_pass(V, 2)
 
     def kv_copy(p):
         return remote(kvs.at[p, theirs], kvr.at[p], kv_sem.at[p], kv_sem.at[2 + p], at(x, y, z, other))
@@ -189,16 +199,16 @@
     def rows(p, zz):
         return W[p, pl.ds(2 * zz, 2)].reshape(BLK, HD)
 
-    for p in range(2):
-        for r in range(2):
-            for sub in range(2):
-                ag_arrival(p, r, sub, 4, sub)
+    def project(p):
+        ag_pass(p, 3)
+        ag_pass(p, 4)
         acc = jnp.zeros((2 * TOK, HD), F32)
         for zz in range(NZ):
             acc += dot(X[zz], rows(p, zz))
         kvs[p] = acc
         kv_copy(p).start()
 
+    project(K)
     small[2].wait()
     seg_t = jnp.broadcast_to(seg[...].astype(F32), (TOK, TOK))
     seg_s = seg_t.T
@@ -230,6 +240,100 @@
     G[V, mine] = gv.astype(BF16)
     g_copy(V).start()
 
+    project(V)
+
+    H = TOK
+
+    def partial(p, r, places):
+        i = (pos[r] + places + 8) % 8
+        if r == 0:
+            lhs = XT[pl.ds(2 * i, 2), :, 0]
+        else:
+            lhs = XT[:, i, 1]
+        return dot(lhs.reshape(2 * TOK, 2 * TOK), G[p])
+
+    def rs_copy(p, r, d, n, sub, places):
+        return remote(
+            SB.at[p, r, d, n, sub], RB.at[p, r, d, n, sub],
+            rs_send.at[p], rs_recv.at[p, r, d, n, sub], neighbour(r, (1 - 2 * d) * places),
+        )
+
+    def rs_out(p, r, d, n, sub, places, value):
+        SB[p, r, d, n, sub] = value.astype(BF16)
+        rs_copy(p, r, d, n, sub, places).start()
+
+    def rs_in(p, r, d, n, sub):
+        wait_bytes(RB.at[p, r, d, n, sub], rs_recv.at[p, r, d, n, sub])
+        return RB[p, r, d, n, sub].astype(F32)
+
+    def rs_begin(p):
+        for r in range(2):
+            part = partial(p, r, 4)
+            for d in range(2):
+                rs_out(p, r, d, 0, d, 2, part[d * H:(d + 1) * H])
+        for r in range(2):
+            for d in range(2):
+                part = partial(p, r, 3 * (1 - 2 * d))
+                for sub in range(2):
+                    rs_out(p, r, d, 1, sub, 1, part[sub * H:(sub + 1) * H])
+
+    def rs_middle(p, n, places):
+        for r in range(2):
+            for d in range(2):
+                part = partial(p, r, 2 * (1 - 2 * d))
+                for sub in range(2):
+                    value = part[sub * H:(sub + 1) * H] + rs_in(p, r, d, 1, sub)
+                    if sub == d:
+                        value += rs_in(p, r, d, 0, sub)
+                    rs_out(p, r, d, n, sub, places, value)
+
+    def rs_near(p, n, arrived=None):
+        for r in range(2):
+            for d in range(2):
+                part = partial(p, r, 1 - 2 * d)
+                for sub in range(2):
+                    value = part[sub * H:(sub + 1) * H]
+                    if arrived is not None:
+                        value += rs_in(p, r, d, arrived, sub)
+                    rs_out(p, r, d, n, sub, 1, value)
+
+    def rs_own(p, arrivals):
+        for r in range(2):
+            own = partial(p, r, 0)
+            for sub in range(2):
+                total = own[sub * H:(sub + 1) * H]
+                for d in range(2):
+                    for n in arrivals:
+                        total += rs_in(p, r, d, n, sub)
+                YS[r, pl.ds(sub * 8, 8), p] = total.astype(BF16).reshape(8, 16, HD)
+
+    def rs_direct(p):
+        for kk in FAR:
+            for r in range(2):
+                for xh in range(2):
+                    if r == 0:
+                        src = YS.at[0, xh * 8 + (y + kk) % NY, p]
+                        dst = XR.at[x * 8 + y, p]
+                    else:
+                        src = YS.at[1, (z + kk) % NZ * 2 + xh, p]
+                        dst = XR.at[x * 8 + z, p]
+                    cp = remote(src, dst, rs_d_send.at[p], rs_d_recv.at[p], owner(r, xh, kk))
+                    if kk == 0:
+                        is_me = (r == c) & (c * 2 + xh == x)
+
+                        @pl.when(jnp.logical_not(is_me))
+                        def _():
+                            cp.start()
+
+                        @pl.when(is_me)
+                        def _():
+                            pltpu.make_async_copy(src, dst, rs_d_recv.at[p]).start()
+                    else:
+                        cp.start()
+
+    wait_bytes(G.at[V, theirs], g_sem.at[2 + V])
+    rs_begin(V)
+
     kv_copy(V).wait_recv()
     vb = (kvs[V, mine] + kvr[V]).astype(BF16)
     gk = jnp.zeros((TOK, HD), F32)
@@ -242,19 +346,6 @@
     G[K, mine] = gk.astype(BF16)
     g_copy(K).start()
 
-    def partial(p, r, i):
-        if r == 0:
-            lhs = XT[pl.ds(2 * i, 2), :, 0]
-        else:
-            lhs = XT[:, i, 1]
-        return dot(lhs.reshape(2 * TOK, 2 * TOK), G[p])
-
-    def rs_copy(p, r, d, s, sub):
-        return remote(
-            SB.at[p, r, d, s - 1, sub], RB.at[p, r, d, s - 1, sub],
-            rs_send.at[p], rs_recv.at[p, r, d, s - 1, sub], neighbour(r, 1 - 2 * d),
-        )
-
     def grad_tokens(zz):
         wz = jnp.concatenate([rows(K, zz), rows(V, zz)], axis=1)
         g = jnp.concatenate([G[K], G[V]], axis=1)
@@ -265,73 +356,22 @@
     def attend_out(h):
         attn[:, h * HD:(h + 1) * HD] = dot(low_s[h // 2, :, h % 2 * TOK:(h % 2 + 1) * TOK], vb, TN).astype(BF16)
 
-    H = TOK
-    for p in (V, K):
-        wait_bytes(G.at[p, theirs], g_sem.at[2 + p])
-        for r in range(2):
-            part = partial(p, r, (pos[r] + 4) % 8).astype(BF16)
-            for d in range(2):
-                SB[p, r, d, 0, d] = part[d * H:(d + 1) * H]
-                rs_copy(p, r, d, 1, d).start()
-    for s in range(2, 5):
-        for p in (V, K):
-            parts = {}
-            for r in range(2):
-                for d in range(2):
-                    step = 1 - 2 * d
-                    parts[r, d] = partial(p, r, (pos[r] + step * (5 - s) + 8) % 8)
-                    if s == 2:
-                        sub = 1 - d
-                        SB[p, r, d, s - 1, sub] = parts[r, d][sub * H:(sub + 1) * H].astype(BF16)
-                        rs_copy(p, r, d, s, sub).start()
-            for sub in range(2):
-                for r in range(2):
-                    for d in range(2):
-                        if s == 2 and sub != d:
-                            continue
-                        rs_copy(p, r, d, s - 1, sub).wait_recv()
-                        add = parts[r, d][sub * H:(sub + 1) * H] + RB[p, r, d, s - 2, sub].astype(F32)
-                        SB[p, r, d, s - 1, sub] = add.astype(BF16)
-                        rs_copy(p, r, d, s, sub).start()
-            half = 0 if p == V else 1
-            if s == 2:
-                for h in range(half * 4, half * 4 + 4):
-                    attend_out(h)
-            else:
-                for zz in range((s - 3) * 4 + half * 2, (s - 3) * 4 + half * 2 + 2):
-                    grad_tokens(zz)
-
-    for p in (V, K):
-        for r in range(2):
-            own = partial(p, r, pos[r])
-            for sub in range(2):
-                total = own[sub * H:(sub + 1) * H]
-                for d in range(2):
-                    rs_copy(p, r, d, 4, sub).wait_recv()
-                    total += RB[p, r, d, 3, sub].astype(F32)
-                YS[r, pl.ds(sub * 8, 8), p] = total.astype(BF16).reshape(8, 16, HD)
-    for kk in FAR:
-        for r in range(2):
-            for xh in range(2):
-                if r == 0:
-                    src = YS.at[0, xh * 8 + (y + kk) % NY]
-                    dst = XR.at[x * 8 + y]
-                else:
-                    src = YS.at[1, (z + kk) % NZ * 2 + xh]
-                    dst = XR.at[x * 8 + z]
-                cp = remote(src, dst, rs_d_send, rs_d_recv, owner(r, xh, kk))
-                if kk == 0:
-                    is_me = (r == c) & (c * 2 + xh == x)
-
-                    @pl.when(jnp.logical_not(is_me))
-                    def _():
-                        cp.start()
-
-                    @pl.when(is_me)
-                    def _():
-                        pltpu.make_async_copy(src, dst, rs_d_recv).start()
-                else:
-                    cp.start()
+    for h in range(GH):
+        attend_out(h)
+    wait_bytes(G.at[K, theirs], g_sem.at[2 + K])
+    rs_begin(K)
+    rs_near(K, 2)
+    rs_middle(V, 2, 1)
+    for zz in range(4):
+        grad_tokens(zz)
+    rs_near(V, 3, 2)
+    rs_middle(K, 3, 2)
+    for zz in range(4, NZ):
+        grad_tokens(zz)
+    rs_own(V, (3,))
+    rs_direct(V)
+    rs_own(K, (2, 3))
+    rs_direct(K)
 
     for k in range(2):
         wait_bytes(gtok.at[:, pl.ds(0, HALF)], gt_sem.at[k])
@@ -350,17 +390,19 @@
     def _():
         wait_bytes(XR, ag_d_send)
 
-    wait_bytes(XR, rs_d_recv)
-    for p in range(2):
+    for p in (V, K):
+        wait_bytes(XR.at[:, p], rs_d_recv.at[p])
         gw[:, p * HD:(p + 1) * HD] = jnp.sum(XR[:, p].astype(F32), axis=0)
 
     @pl.when(home == c)
     def _():
-        wait_bytes(XR.at[pl.ds(0, 31)], rs_d_send)
+        for p in range(2):
+            wait_bytes(XR.at[pl.ds(0, 31), p], rs_d_send.at[p])
 
     @pl.when(home != c)
     def _():
-        wait_bytes(XR, rs_d_send)
+        for p in range(2):
+            wait_bytes(XR.at[:, p], rs_d_send.at[p])
 
 
 OUTS = (((TOK, GH * HD), BF16), ((TOK, D), BF16), ((16, 2 * HD), F32))
@@ -404,7 +446,7 @@
             pltpu.VMEM((2, 16, 2, 16, HD), BF16),
             pltpu.VMEM((32, 2, 16, HD), BF16),
             dma((6,)), dma((2,)), dma, dma((2,)), dma((2,)), dma((2, 2, 2, 4, 2)),
-            dma((4,)), dma((4,)), dma((2,)), dma((2,)), dma((2, 2, 2, 4, 2)), dma, dma,
+            dma((4,)), dma((4,)), dma((2,)), dma((2,)), dma((2, 2, 2, 4, 2)), dma((2,)), dma((2,)),
         ],
         compiler_params=pltpu.CompilerParams(
             collective_id=0, has_side_effects=True, vmem_limit_bytes=60 * 2**20
@@ -418,6 +460,7 @@
         in_specs=[vmem] * 3,
         out_specs=(pl.BlockSpec(memory_space=pl.ANY),) * 3,
         scratch_shapes=[dma((3,))],
+        compiler_params=pltpu.CompilerParams(vmem_limit_bytes=4 * 2**20),
         name="write_out",
     )(*inner))
 

time: 73.5 us -> 69.9 us (0.951)
  local copies, waits for them, and re-layouts: 2.64 us -> 0 us
  Pallas kernels: 70.1 us -> 69.1 us
    unnamed x6 -> x0, local copies, waits for them, and re-layouts: 2.64 us -> none
    pallas_call x1, Pallas kernels: 3.02 us -> 1.44 us  [shards(): pl.pallas_call(write_out, out_shape=tuple((jax.ShapeDtypeStruct(shape, dt...]
where the time goes in v4:
time: 69.9 us; the launch traced here: 69.8 us
  Pallas kernels  69.1 us (99%)
    pallas_call x1, Pallas kernels, shards(): pl.pallas_call(kernel, out_shape=tuple((pltpu.VMEM(shape, dtype) for shap...  67.7 us
    pallas_call x1, Pallas kernels, shards(): pl.pallas_call(write_out, out_shape=tuple((jax.ShapeDtypeStruct(shape, dt...  1.44 us

profile of v4, /device:TPU:1, one launch (start us, length us, event | category | flops | bytes accessed | tf_op | source)
XLA Modules:
  0.0 69.8 jit_solution(1150037285746390080)
XLA Ops:
  0.6 67.7 %layer.1 = (bf16[128,1024]{1,0:T(8,128)(2,1)S(1)}, bf16[128,8192]{1,0:T(8,128)(2,1)S(1)}, f32[16,256]{1,0:T(8,128)S(1)}) custom-call(bf16[128,8192]{1,0:T(8,128)(2,1)} %tok.1, bf16[128,1024]{1,0:T(8,128)(2,1)} %q_hbm.1, bf16[128,1024]{1,0:T(8,128)(2,1)} %go_hbm.1, s32[1,128]{1,0:T(1,128)} %seg_hbm.1, bf16[16,256]{1,0:T(8,128)(2,1)} %w_hbm.1, ...), custom_call_target="tpu_custom_call" | custom-call | flops 2000000000 | bytes 5242880 | tf_op jit(solution)/shard_map/layer/pallas_call | solution.py:423
  68.3 1.4 %write_out.1 = (bf16[128,1024]{1,0:T(8,128)(2,1)}, bf16[128,8192]{1,0:T(8,128)(2,1)}, f32[16,256]{1,0:T(8,128)}) custom-call(bf16[128,1024]{1,0:T(8,128)(2,1)S(1)} %get-tuple-element.6.refs_0_, bf16[128,8192]{1,0:T(8,128)(2,1)S(1)} %get-tuple-element.7.refs_1_, f32[16,256]{1,0:T(8,128)S(1)} %get-tuple-element.8.refs_2_), custom_call_target="tpu_custom_call" | custom-call | tf_op jit(solution)/shard_map/write_out/pallas_call | solution.py:457

commit v5 on v4

--- a/solution.py
+++ b/solution.py
@@ -166,7 +166,7 @@
     def ag_arrival(p, r, d, k, sub):
         wait_bytes(piece(p, r, (pos[r] - (1 - 2 * d) * k + 8) % 8, sub), ag_recv.at[p, r, d, k - 1, sub])
 
-    GOES = ({0: (2, 1), 2: (2, 1)}, {0: (1,), 1: (1,), 2: (2, 1)})
+    GOES = ({0: (1,), 1: (1,), 2: (2, 1)},) * 2
 
     def ag_pass(p, k):
         for sub in range(2):
@@ -186,11 +186,11 @@
     ag_pass(V, 0)
     for zz in range(4, 6):
         turn(zz)
-    ag_pass(K, 2)
+    ag_pass(K, 1)
     ag_pass(V, 1)
     for zz in range(6, 8):
         turn(zz)
-    ag_pass(K, 1)
+    ag_pass(K, 2)
     ag_pass(V, 2)
 
     def kv_copy(p):
@@ -356,21 +356,21 @@
     def attend_out(h):
         attn[:, h * HD:(h + 1) * HD] = dot(low_s[h // 2, :, h % 2 * TOK:(h % 2 + 1) * TOK], vb, TN).astype(BF16)
 
+    wait_bytes(G.at[K, theirs], g_sem.at[2 + K])
+    rs_begin(K)
+    rs_middle(V, 2, 1)
     for h in range(GH):
         attend_out(h)
-    wait_bytes(G.at[K, theirs], g_sem.at[2 + K])
-    rs_begin(K)
-    rs_near(K, 2)
-    rs_middle(V, 2, 1)
+    rs_middle(K, 2, 1)
     for zz in range(4):
         grad_tokens(zz)
     rs_near(V, 3, 2)
-    rs_middle(K, 3, 2)
+    rs_near(K, 3, 2)
     for zz in range(4, NZ):
         grad_tokens(zz)
     rs_own(V, (3,))
     rs_direct(V)
-    rs_own(K, (2, 3))
+    rs_own(K, (3,))
     rs_direct(K)
 
     for k in range(2):

time: 69.9 us -> 65.8 us (0.941)
  Pallas kernels: 69.1 us -> 65 us
    pallas_call x1, Pallas kernels: 67.7 us -> 63.6 us  [shards(): pl.pallas_call(kernel, out_shape=tuple((pltpu.VMEM(shape, dtype) for shap...]
where the time goes in v5:
time: 65.8 us; the launch traced here: 65.6 us
  Pallas kernels  65 us (99%)
    pallas_call x1, Pallas kernels, shards(): pl.pallas_call(kernel, out_shape=tuple((pltpu.VMEM(shape, dtype) for shap...  63.6 us
    pallas_call x1, Pallas kernels, shards(): pl.pallas_call(write_out, out_shape=tuple((jax.ShapeDtypeStruct(shape, dt...  1.44 us

profile of v5, /device:TPU:1, one launch (start us, length us, event | category | flops | bytes accessed | tf_op | source)
XLA Modules:
  0.0 65.6 jit_solution(12162666117111574524)
XLA Ops:
  0.6 63.6 %layer.1 = (bf16[128,1024]{1,0:T(8,128)(2,1)S(1)}, bf16[128,8192]{1,0:T(8,128)(2,1)S(1)}, f32[16,256]{1,0:T(8,128)S(1)}) custom-call(bf16[128,8192]{1,0:T(8,128)(2,1)} %tok.1, bf16[128,1024]{1,0:T(8,128)(2,1)} %q_hbm.1, bf16[128,1024]{1,0:T(8,128)(2,1)} %go_hbm.1, s32[1,128]{1,0:T(1,128)} %seg_hbm.1, bf16[16,256]{1,0:T(8,128)(2,1)} %w_hbm.1, ...), custom_call_target="tpu_custom_call" | custom-call | flops 2000000000 | bytes 5242880 | tf_op jit(solution)/shard_map/layer/pallas_call | solution.py:423
  64.2 1.4 %write_out.1 = (bf16[128,1024]{1,0:T(8,128)(2,1)}, bf16[128,8192]{1,0:T(8,128)(2,1)}, f32[16,256]{1,0:T(8,128)}) custom-call(bf16[128,1024]{1,0:T(8,128)(2,1)S(1)} %get-tuple-element.6.refs_0_, bf16[128,8192]{1,0:T(8,128)(2,1)S(1)} %get-tuple-element.7.refs_1_, f32[16,256]{1,0:T(8,128)S(1)} %get-tuple-element.8.refs_2_), custom_call_target="tpu_custom_call" | custom-call | tf_op jit(solution)/shard_map/write_out/pallas_call | solution.py:457

commit v6 on v5

--- a/solution.py
+++ b/solution.py
@@ -34,7 +34,7 @@
 def kernel(
     tok, q_hbm, go_hbm, seg_hbm, w_hbm, scales_hbm,
     attn, gtok, gw,
-    seg, w, scales, X, XT, W, GT, qv, gov, prob_s, low_s, sh, kvs, kvr, G, SB, RB, YS, XR,
+    seg, w, scales, X, XT, W, GT, qv, gov, prob_s, low_s, sh, kvs, kvr, G, PB, SB, RB, YS, XR,
     l_sem, tok_sem, ag_d_send, ag_d_recv, ag_send, ag_recv,
     kv_sem, g_sem, gt_sem, rs_send, rs_recv, rs_d_send, rs_d_recv,
 ):
@@ -57,6 +57,13 @@
 
     mine = pl.ds(pl.multiple_of(c * TOK, TOK), TOK)
     theirs = pl.ds(pl.multiple_of(other * TOK, TOK), TOK)
+
+    small = [
+        pltpu.make_async_copy(src, dst, l_sem.at[3 + n])
+        for n, (src, dst) in enumerate(((w_hbm, w), (scales_hbm, scales), (seg_hbm, seg)))
+    ]
+    for copy in small:
+        copy.start()
 
     bar = pltpu.get_barrier_semaphore()
 
@@ -90,12 +97,6 @@
         greet(at(x, y, (z + step) % NZ, c))
     greet(at(x, y, z, other))
 
-    small = [
-        pltpu.make_async_copy(src, dst, l_sem.at[3 + n])
-        for n, (src, dst) in enumerate(((w_hbm, w), (scales_hbm, scales), (seg_hbm, seg)))
-    ]
-    for copy in small:
-        copy.start()
     for zz in range(NZ):
         pltpu.make_async_copy(tok.at[:, cols(zz, c)], X.at[zz, mine], l_sem.at[0]).start()
     q_copy = pltpu.make_async_copy(q_hbm, qv, l_sem.at[1])
@@ -231,7 +232,7 @@
     for h in range(0, GH, 2):
         st = jnp.where(allowed, dot(kb, pair(qv, h), NT) * SCALE, -1e30)
         top = jnp.max(st, axis=0, keepdims=True)
-        ex = jnp.where(allowed, jnp.exp(st - top), 0.0)
+        ex = jnp.exp(st - top)
         pr = ex * (1.0 / jnp.sum(ex, axis=0, keepdims=True))
         low = pr.astype(BF16)
         prob_s[h // 2] = pr
@@ -277,59 +278,55 @@
                 for sub in range(2):
                     rs_out(p, r, d, 1, sub, 1, part[sub * H:(sub + 1) * H])
 
-    def rs_middle(p, n, places):
+    def rs_ahead(p):
         for r in range(2):
-            for d in range(2):
-                part = partial(p, r, 2 * (1 - 2 * d))
-                for sub in range(2):
-                    value = part[sub * H:(sub + 1) * H] + rs_in(p, r, d, 1, sub)
+            for n, places in enumerate((2, -2, 1, -1, 0)):
+                PB[p, r, n] = partial(p, r, places)
+
+    def rs_middle(p):
+        for sub in range(2):
+            for r in range(2):
+                for d in range(2):
+                    value = PB[p, r, d, sub * H:(sub + 1) * H] + rs_in(p, r, d, 1, sub)
                     if sub == d:
                         value += rs_in(p, r, d, 0, sub)
-                    rs_out(p, r, d, n, sub, places, value)
-
-    def rs_near(p, n, arrived=None):
-        for r in range(2):
+                    rs_out(p, r, d, 2, sub, 1, value)
+
+    def rs_near(p):
+        for sub in range(2):
+            for r in range(2):
+                for d in range(2):
+                    rs_out(p, r, d, 3, sub, 1, PB[p, r, 2 + d, sub * H:(sub + 1) * H] + rs_in(p, r, d, 2, sub))
+
+    def rs_own(p, r):
+        for sub in range(2):
+            total = PB[p, r, 4, sub * H:(sub + 1) * H]
             for d in range(2):
-                part = partial(p, r, 1 - 2 * d)
-                for sub in range(2):
-                    value = part[sub * H:(sub + 1) * H]
-                    if arrived is not None:
-                        value += rs_in(p, r, d, arrived, sub)
-                    rs_out(p, r, d, n, sub, 1, value)
-
-    def rs_own(p, arrivals):
-        for r in range(2):
-            own = partial(p, r, 0)
-            for sub in range(2):
-                total = own[sub * H:(sub + 1) * H]
-                for d in range(2):
-                    for n in arrivals:
-                        total += rs_in(p, r, d, n, sub)
-                YS[r, pl.ds(sub * 8, 8), p] = total.astype(BF16).reshape(8, 16, HD)
-
-    def rs_direct(p):
+                total += rs_in(p, r, d, 3, sub)
+            YS[r, pl.ds(sub * 8, 8), p] = total.astype(BF16).reshape(8, 16, HD)
+
+    def rs_direct(p, r):
         for kk in FAR:
-            for r in range(2):
-                for xh in range(2):
-                    if r == 0:
-                        src = YS.at[0, xh * 8 + (y + kk) % NY, p]
-                        dst = XR.at[x * 8 + y, p]
-                    else:
-                        src = YS.at[1, (z + kk) % NZ * 2 + xh, p]
-                        dst = XR.at[x * 8 + z, p]
-                    cp = remote(src, dst, rs_d_send.at[p], rs_d_recv.at[p], owner(r, xh, kk))
-                    if kk == 0:
-                        is_me = (r == c) & (c * 2 + xh == x)
-
-                        @pl.when(jnp.logical_not(is_me))
-                        def _():
-                            cp.start()
-
-                        @pl.when(is_me)
-                        def _():
-                            pltpu.make_async_copy(src, dst, rs_d_recv.at[p]).start()
-                    else:
+            for xh in range(2):
+                if r == 0:
+                    src = YS.at[0, xh * 8 + (y + kk) % NY, p]
+                    dst = XR.at[x * 8 + y, p]
+                else:
+                    src = YS.at[1, (z + kk) % NZ * 2 + xh, p]
+                    dst = XR.at[x * 8 + z, p]
+                cp = remote(src, dst, rs_d_send.at[p], rs_d_recv.at[p], owner(r, xh, kk))
+                if kk == 0:
+                    is_me = (r == c) & (c * 2 + xh == x)
+
+                    @pl.when(jnp.logical_not(is_me))
+                    def _():
                         cp.start()
+
+                    @pl.when(is_me)
+                    def _():
+                        pltpu.make_async_copy(src, dst, rs_d_recv.at[p]).start()
+                else:
+                    cp.start()
 
     wait_bytes(G.at[V, theirs], g_sem.at[2 + V])
     rs_begin(V)
@@ -356,22 +353,26 @@
     def attend_out(h):
         attn[:, h * HD:(h + 1) * HD] = dot(low_s[h // 2, :, h % 2 * TOK:(h % 2 + 1) * TOK], vb, TN).astype(BF16)
 
+    rs_ahead(V)
     wait_bytes(G.at[K, theirs], g_sem.at[2 + K])
     rs_begin(K)
-    rs_middle(V, 2, 1)
+    rs_middle(V)
+    rs_ahead(K)
+    rs_middle(K)
+    rs_near(V)
+    for zz in range(0, 4):
+        grad_tokens(zz)
+    rs_near(K)
+    for zz in range(4, 8):
+        grad_tokens(zz)
+    for r in range(2):
+        rs_own(V, r)
+        rs_direct(V, r)
+    for r in range(2):
+        rs_own(K, r)
+        rs_direct(K, r)
     for h in range(GH):
         attend_out(h)
-    rs_middle(K, 2, 1)
-    for zz in range(4):
-        grad_tokens(zz)
-    rs_near(V, 3, 2)
-    rs_near(K, 3, 2)
-    for zz in range(4, NZ):
-        grad_tokens(zz)
-    rs_own(V, (3,))
-    rs_direct(V)
-    rs_own(K, (3,))
-    rs_direct(K)
 
     for k in range(2):
         wait_bytes(gtok.at[:, pl.ds(0, HALF)], gt_sem.at[k])
@@ -441,6 +442,7 @@
             pltpu.VMEM((2, 2 * TOK, HD), F32),
             pltpu.VMEM((2, TOK, HD), F32),
             pltpu.VMEM((2, 2 * TOK, HD), BF16),
+            pltpu.VMEM((2, 2, 5, 2 * TOK, HD), F32),
             pltpu.VMEM((2, 2, 2, 4, 2, TOK, HD), BF16),
             pltpu.VMEM((2, 2, 2, 4, 2, TOK, HD), BF16),
             pltpu.VMEM((2, 16, 2, 16, HD), BF16),

time: 65.8 us -> 64.7 us (0.983)
  Pallas kernels: 65 us -> 63.9 us
    pallas_call x1, Pallas kernels: 63.6 us -> 62.5 us  [shards(): pl.pallas_call(kernel, out_shape=tuple((pltpu.VMEM(shape, dtype) for shap...]
where the time goes in v6:
time: 64.7 us; the launch traced here: 64.6 us
  Pallas kernels  63.9 us (99%)
    pallas_call x1, Pallas kernels, shards(): pl.pallas_call(kernel, out_shape=tuple((pltpu.VMEM(shape, dtype) for shap...  62.5 us
    pallas_call x1, Pallas kernels, shards(): pl.pallas_call(write_out, out_shape=tuple((jax.ShapeDtypeStruct(shape, dt...  1.44 us

profile of v6, /device:TPU:1, one launch (start us, length us, event | category | flops | bytes accessed | tf_op | source)
XLA Modules:
  0.0 64.6 jit_solution(18175898160445508010)
XLA Ops:
  0.6 62.5 %layer.1 = (bf16[128,1024]{1,0:T(8,128)(2,1)S(1)}, bf16[128,8192]{1,0:T(8,128)(2,1)S(1)}, f32[16,256]{1,0:T(8,128)S(1)}) custom-call(bf16[128,8192]{1,0:T(8,128)(2,1)} %tok.1, bf16[128,1024]{1,0:T(8,128)(2,1)} %q_hbm.1, bf16[128,1024]{1,0:T(8,128)(2,1)} %go_hbm.1, s32[1,128]{1,0:T(1,128)} %seg_hbm.1, bf16[16,256]{1,0:T(8,128)(2,1)} %w_hbm.1, ...), custom_call_target="tpu_custom_call" | custom-call | flops 2000000000 | bytes 5242880 | tf_op jit(solution)/shard_map/layer/pallas_call | solution.py:424
  63.1 1.4 %write_out.1 = (bf16[128,1024]{1,0:T(8,128)(2,1)}, bf16[128,8192]{1,0:T(8,128)(2,1)}, f32[16,256]{1,0:T(8,128)}) custom-call(bf16[128,1024]{1,0:T(8,128)(2,1)S(1)} %get-tuple-element.6.refs_0_, bf16[128,8192]{1,0:T(8,128)(2,1)S(1)} %get-tuple-element.7.refs_1_, f32[16,256]{1,0:T(8,128)S(1)} %get-tuple-element.8.refs_2_), custom_call_target="tpu_custom_call" | custom-call | tf_op jit(solution)/shard_map/write_out/pallas_call | solution.py:459

commit v7 on v6

--- a/solution.py
+++ b/solution.py
@@ -203,11 +203,13 @@
     def project(p):
         ag_pass(p, 3)
         ag_pass(p, 4)
-        acc = jnp.zeros((2 * TOK, HD), F32)
-        for zz in range(NZ):
-            acc += dot(X[zz], rows(p, zz))
-        kvs[p] = acc
-        kv_copy(p).start()
+        for part in (theirs, mine):
+            acc = jnp.zeros((TOK, HD), F32)
+            for zz in range(NZ):
+                acc += dot(X[zz, part], rows(p, zz))
+            kvs[p, part] = acc
+            if part is theirs:
+                kv_copy(p).start()
 
     project(K)
     small[2].wait()
@@ -216,28 +218,25 @@
     s_at = lax.broadcasted_iota(jnp.int32, (TOK, TOK), 0)
     t_at = lax.broadcasted_iota(jnp.int32, (TOK, TOK), 1)
     one = jnp.where((s_at <= t_at) & (seg_s == seg_t), 1.0, 0.0)
-    allowed = jnp.concatenate([one, one], axis=1) > 0.5
+    allowed = jnp.concatenate([one] * GH, axis=1) > 0.5
     q_copy.wait()
     go_copy.wait()
 
-    def pair(ref, h):
-        return jnp.concatenate([ref[:, h * HD:(h + 1) * HD], ref[:, (h + 1) * HD:(h + 2) * HD]], axis=0)
+    def stacked(ref):
+        return jnp.concatenate([ref[:, h * HD:(h + 1) * HD] for h in range(GH)], axis=0)
 
     def g_copy(p):
         return remote(G.at[p, mine], G.at[p, mine], g_sem.at[p], g_sem.at[2 + p], at(x, y, z, other))
 
     kv_copy(K).wait_recv()
     kb = (kvs[K, mine] + kvr[K]).astype(BF16)
-    gv = jnp.zeros((TOK, HD), F32)
-    for h in range(0, GH, 2):
-        st = jnp.where(allowed, dot(kb, pair(qv, h), NT) * SCALE, -1e30)
-        top = jnp.max(st, axis=0, keepdims=True)
-        ex = jnp.exp(st - top)
-        pr = ex * (1.0 / jnp.sum(ex, axis=0, keepdims=True))
-        low = pr.astype(BF16)
-        prob_s[h // 2] = pr
-        low_s[h // 2] = low
-        gv += dot(low, pair(gov, h))
+    st = jnp.where(allowed, dot(kb, stacked(qv), NT) * SCALE, -1e30)
+    ex = jnp.exp(st - jnp.max(st, axis=0, keepdims=True))
+    pr = ex * (1.0 / jnp.sum(ex, axis=0, keepdims=True))
+    low = pr.astype(BF16)
+    prob_s[...] = pr
+    low_s[...] = low
+    gv = dot(low, stacked(gov))
     G[V, mine] = gv.astype(BF16)
     g_copy(V).start()
 
@@ -333,13 +332,10 @@
 
     kv_copy(V).wait_recv()
     vb = (kvs[V, mine] + kvr[V]).astype(BF16)
-    gk = jnp.zeros((TOK, HD), F32)
-    for h in range(0, GH, 2):
-        pr = prob_s[h // 2]
-        dp = dot(vb, pair(gov, h), NT)
-        inner = jnp.sum(pr * dp, axis=0, keepdims=True)
-        ds = (pr * (dp - inner) * SCALE).astype(BF16)
-        gk += dot(ds, pair(qv, h))
+    pr = prob_s[...]
+    dp = dot(vb, stacked(gov), NT)
+    inner = jnp.sum(pr * dp, axis=0, keepdims=True)
+    gk = dot((pr * (dp - inner) * SCALE).astype(BF16), stacked(qv))
     G[K, mine] = gk.astype(BF16)
     g_copy(K).start()
 
@@ -351,7 +347,7 @@
         remote(GT.at[zz, theirs], gtok.at[:, cols(zz, c)], gt_sem.at[0], gt_sem.at[1], at(x, y, z, other)).start()
 
     def attend_out(h):
-        attn[:, h * HD:(h + 1) * HD] = dot(low_s[h // 2, :, h % 2 * TOK:(h % 2 + 1) * TOK], vb, TN).astype(BF16)
+        attn[:, h * HD:(h + 1) * HD] = dot(low_s[:, h * TOK:(h + 1) * TOK], vb, TN).astype(BF16)
 
     rs_ahead(V)
     wait_bytes(G.at[K, theirs], g_sem.at[2 + K])
@@ -436,8 +432,8 @@
             pltpu.VMEM((NZ, 2 * TOK, BLK), BF16),
             pltpu.VMEM((TOK, GH * HD), BF16),
             pltpu.VMEM((TOK, GH * HD), BF16),
-            pltpu.VMEM((GH // 2, TOK, 2 * TOK), F32),
-            pltpu.VMEM((GH // 2, TOK, 2 * TOK), BF16),
+            pltpu.VMEM((TOK, GH * TOK), F32),
+            pltpu.VMEM((TOK, GH * TOK), BF16),
             pltpu.VMEM((2, 16, HD), BF16),
             pltpu.VMEM((2, 2 * TOK, HD), F32),
             pltpu.VMEM((2, TOK, HD), F32),

time: 64.7 us -> 64.5 us (level)
  no operation moved by 1% of the time
where the time goes in v7:
time: 64.5 us; the launch traced here: 64.3 us
  Pallas kernels  63.7 us (99%)
    pallas_call x1, Pallas kernels, shards(): pl.pallas_call(kernel, out_shape=tuple((pltpu.VMEM(shape, dtype) for shap...  62.3 us
    pallas_call x1, Pallas kernels, shards(): pl.pallas_call(write_out, out_shape=tuple((jax.ShapeDtypeStruct(shape, dt...  1.44 us

profile of v7, /device:TPU:1, one launch (start us, length us, event | category | flops | bytes accessed | tf_op | source)
XLA Modules:
  0.0 64.3 jit_solution(14343028504422031169)
XLA Ops:
  0.6 62.3 %layer.1 = (bf16[128,1024]{1,0:T(8,128)(2,1)S(1)}, bf16[128,8192]{1,0:T(8,128)(2,1)S(1)}, f32[16,256]{1,0:T(8,128)S(1)}) custom-call(bf16[128,8192]{1,0:T(8,128)(2,1)} %tok.1, bf16[128,1024]{1,0:T(8,128)(2,1)} %q_hbm.1, bf16[128,1024]{1,0:T(8,128)(2,1)} %go_hbm.1, s32[1,128]{1,0:T(1,128)} %seg_hbm.1, bf16[16,256]{1,0:T(8,128)(2,1)} %w_hbm.1, ...), custom_call_target="tpu_custom_call" | custom-call | flops 2000000000 | bytes 5242880 | tf_op jit(solution)/shard_map/layer/pallas_call | solution.py:420
  62.9 1.4 %write_out.1 = (bf16[128,1024]{1,0:T(8,128)(2,1)}, bf16[128,8192]{1,0:T(8,128)(2,1)}, f32[16,256]{1,0:T(8,128)}) custom-call(bf16[128,1024]{1,0:T(8,128)(2,1)S(1)} %get-tuple-element.6.refs_0_, bf16[128,8192]{1,0:T(8,128)(2,1)S(1)} %get-tuple-element.7.refs_1_, f32[16,256]{1,0:T(8,128)S(1)} %get-tuple-element.8.refs_2_), custom_call_target="tpu_custom_call" | custom-call | tf_op jit(solution)/shard_map/write_out/pallas_call | solution.py:455

commit v8 on v7

--- a/solution.py
+++ b/solution.py
@@ -135,17 +135,9 @@
             else:
                 cp.start()
 
-    for zz in range(NZ):
-        remote(tok.at[:, cols(zz, other)], X.at[zz, mine], tok_sem.at[0], tok_sem.at[1], at(x, y, z, other)).start()
-
-    wait_bytes(X.at[:, mine], l_sem.at[0])
-    wait_bytes(X.at[:, theirs], tok_sem.at[1])
 
     def turn(zz):
         XT[pl.ds(2 * zz, 2)] = X[zz].T.reshape(2, NY, 2, 16, 2 * TOK)
-
-    for zz in range(4):
-        turn(zz)
 
     def piece(p, r, i, sub):
         if r == 0:
@@ -185,14 +177,19 @@
     wait_bytes(W.at[:, :, y, 1], ag_d_recv.at[1])
     ag_pass(K, 0)
     ag_pass(V, 0)
-    for zz in range(4, 6):
-        turn(zz)
+
+    for zz in range(NZ):
+        remote(tok.at[:, cols(zz, other)], X.at[zz, mine], tok_sem.at[0], tok_sem.at[1], at(x, y, z, other)).start()
     ag_pass(K, 1)
     ag_pass(V, 1)
-    for zz in range(6, 8):
+    wait_bytes(X.at[:, mine], l_sem.at[0])
+    wait_bytes(X.at[:, theirs], tok_sem.at[1])
+    for zz in range(4):
         turn(zz)
     ag_pass(K, 2)
     ag_pass(V, 2)
+    for zz in range(4, NZ):
+        turn(zz)
 
     def kv_copy(p):
         return remote(kvs.at[p, theirs], kvr.at[p], kv_sem.at[p], kv_sem.at[2 + p], at(x, y, z, other))
@@ -304,16 +301,16 @@
                 total += rs_in(p, r, d, 3, sub)
             YS[r, pl.ds(sub * 8, 8), p] = total.astype(BF16).reshape(8, 16, HD)
 
-    def rs_direct(p, r):
+    def rs_direct(r):
         for kk in FAR:
             for xh in range(2):
                 if r == 0:
-                    src = YS.at[0, xh * 8 + (y + kk) % NY, p]
-                    dst = XR.at[x * 8 + y, p]
+                    src = YS.at[0, xh * 8 + (y + kk) % NY]
+                    dst = XR.at[x * 8 + y]
                 else:
-                    src = YS.at[1, (z + kk) % NZ * 2 + xh, p]
-                    dst = XR.at[x * 8 + z, p]
-                cp = remote(src, dst, rs_d_send.at[p], rs_d_recv.at[p], owner(r, xh, kk))
+                    src = YS.at[1, (z + kk) % NZ * 2 + xh]
+                    dst = XR.at[x * 8 + z]
+                cp = remote(src, dst, rs_d_send, rs_d_recv, owner(r, xh, kk))
                 if kk == 0:
                     is_me = (r == c) & (c * 2 + xh == x)
 
@@ -323,7 +320,7 @@
 
                     @pl.when(is_me)
                     def _():
-                        pltpu.make_async_copy(src, dst, rs_d_recv.at[p]).start()
+                        pltpu.make_async_copy(src, dst, rs_d_recv).start()
                 else:
                     cp.start()
 
@@ -363,10 +360,9 @@
         grad_tokens(zz)
     for r in range(2):
         rs_own(V, r)
-        rs_direct(V, r)
     for r in range(2):
         rs_own(K, r)
-        rs_direct(K, r)
+        rs_direct(r)
     for h in range(GH):
         attend_out(h)
 
@@ -387,19 +383,17 @@
     def _():
         wait_bytes(XR, ag_d_send)
 
-    for p in (V, K):
-        wait_bytes(XR.at[:, p], rs_d_recv.at[p])
+    wait_bytes(XR, rs_d_recv)
+    for p in range(2):
         gw[:, p * HD:(p + 1) * HD] = jnp.sum(XR[:, p].astype(F32), axis=0)
 
     @pl.when(home == c)
     def _():
-        for p in range(2):
-            wait_bytes(XR.at[pl.ds(0, 31), p], rs_d_send.at[p])
+        wait_bytes(XR.at[pl.ds(0, 31)], rs_d_send)
 
     @pl.when(home != c)
     def _():
-        for p in range(2):
-            wait_bytes(XR.at[:, p], rs_d_send.at[p])
+        wait_bytes(XR, rs_d_send)
 
 
 OUTS = (((TOK, GH * HD), BF16), ((TOK, D), BF16), ((16, 2 * HD), F32))
@@ -444,7 +438,7 @@
             pltpu.VMEM((2, 16, 2, 16, HD), BF16),
             pltpu.VMEM((32, 2, 16, HD), BF16),
             dma((6,)), dma((2,)), dma, dma((2,)), dma((2,)), dma((2, 2, 2, 4, 2)),
-            dma((4,)), dma((4,)), dma((2,)), dma((2,)), dma((2, 2, 2, 4, 2)), dma((2,)), dma((2,)),
+            dma((4,)), dma((4,)), dma((2,)), dma((2,)), dma((2, 2, 2, 4, 2)), dma, dma,
         ],
         compiler_params=pltpu.CompilerParams(
             collective_id=0, has_side_effects=True, vmem_limit_bytes=60 * 2**20

time: 64.5 us -> 64.9 us (level)
  no operation moved by 1% of the time
where the time goes in v8:
time: 64.9 us; the launch traced here: 64.8 us
  Pallas kernels  64.1 us (99%)
    pallas_call x1, Pallas kernels, shards(): pl.pallas_call(kernel, out_shape=tuple((pltpu.VMEM(shape, dtype) for shap...  62.7 us
    pallas_call x1, Pallas kernels, shards(): pl.pallas_call(write_out, out_shape=tuple((jax.ShapeDtypeStruct(shape, dt...  1.44 us

profile of v8, /device:TPU:1, one launch (start us, length us, event | category | flops | bytes accessed | tf_op | source)
XLA Modules:
  0.0 64.8 jit_solution(3347117573039680317)
XLA Ops:
  0.6 62.7 %layer.1 = (bf16[128,1024]{1,0:T(8,128)(2,1)S(1)}, bf16[128,8192]{1,0:T(8,128)(2,1)S(1)}, f32[16,256]{1,0:T(8,128)S(1)}) custom-call(bf16[128,8192]{1,0:T(8,128)(2,1)} %tok.1, bf16[128,1024]{1,0:T(8,128)(2,1)} %q_hbm.1, bf16[128,1024]{1,0:T(8,128)(2,1)} %go_hbm.1, s32[1,128]{1,0:T(1,128)} %seg_hbm.1, bf16[16,256]{1,0:T(8,128)(2,1)} %w_hbm.1, ...), custom_call_target="tpu_custom_call" | custom-call | flops 2000000000 | bytes 5242880 | tf_op jit(solution)/shard_map/layer/pallas_call | solution.py:414
  63.4 1.4 %write_out.1 = (bf16[128,1024]{1,0:T(8,128)(2,1)}, bf16[128,8192]{1,0:T(8,128)(2,1)}, f32[16,256]{1,0:T(8,128)}) custom-call(bf16[128,1024]{1,0:T(8,128)(2,1)S(1)} %get-tuple-element.6.refs_0_, bf16[128,8192]{1,0:T(8,128)(2,1)S(1)} %get-tuple-element.7.refs_1_, f32[16,256]{1,0:T(8,128)S(1)} %get-tuple-element.8.refs_2_), custom_call_target="tpu_custom_call" | custom-call | tf_op jit(solution)/shard_map/write_out/pallas_call | solution.py:449
